TPU v7x, 128 devices: a whole 4x4x4 slice. The times are simulated.
128 devices in a mesh: ctx: 128 (over z, x, y, core).
Axes of the slice: x: 4, y: 4, z: 4, core: 2. Of those that a mesh axis runs over, the one named last changes fastest.
Arguments:
- queries: bfloat16 [65536, 2048], P('ctx'), may hold values from -13 to 13
- keys: bfloat16 [65536, 2048], P('ctx'), may hold values from -13 to 13
- values: bfloat16 [65536, 2048], P('ctx'), may hold values from -6 to 6
- chosen: int32 [128, 16, 3], P('ctx'), may hold values from 0 to 127, as said below
Outputs:
- attended: bfloat16 [65536, 2048], P('ctx')
Inputs may be any that keep to these rules, and one draw needn't show every extreme that they name: chosen[b, h, :] are three different blocks, none equal to b; over the 48 entries of one query block no block appears more than 1 times, and some block appears exactly 1 times.
All inputs are finite; a program needn't handle non-finite values.
Results may differ from a plain program's by a relative error of at most 0.0049.
Values may be sent and summed in bfloat16 or wider, within the bound.
No kernel may reach another device: no remote copies, remote signals or barrier semaphores. Data moves between devices by JAX's collectives and lax.ppermute only.
A program may use at most 192 MiB of HBM per device.

v0:
```python
import math

import jax
import jax.numpy as jnp
from jax import lax
from jax.experimental import pallas as pl
from jax.experimental.pallas import tpu as pltpu
from jax.sharding import PartitionSpec as P

HEAD = 128
HEADS = 16
BLOCK = 512
DEVICES = 128
CHIPS = 64
SCALE = math.log2(math.e) / math.sqrt(HEAD)

ONE = [(1, 0, 0), (3, 0, 0), (0, 1, 0), (0, 3, 0), (0, 0, 1), (0, 0, 3)]
PARTNER = 6
SHIFTS = [(0, 0, 0, 1)] * PARTNER
SHIFTS += [(*s, c) for s in ONE for c in (0, 1)]
KINDS = len(SHIFTS)
SPARE = 5
PIECE = 16
WAVES = 4
UP_TO = (8, 12, 15)
WAVE_OF = [1] * (PARTNER + 4) + [2] * 4 + [3] * 4
CODE_PARTNER = CHIPS
CODE_FORWARD = CODE_PARTNER + 1
CODE_SPARE = CODE_FORWARD + KINDS
LIST = 3 * HEADS
COUNT = LIST + WAVES * HEADS
NEED = COUNT + WAVES
TABLE = NEED + 2 * HEADS
HALF = BLOCK // PIECE
SLOT_PIECES = 2 * HALF + SPARE
SLOT_ROWS = SLOT_PIECES * PIECE

ROW_DIRECT = CHIPS
ROW_SPARE = ROW_DIRECT + CHIPS
ROW_FORWARD = ROW_SPARE + CHIPS
ROW_FORWARD_HEAD = ROW_FORWARD + KINDS
ROW_FROM_HEAD = ROW_FORWARD_HEAD + KINDS
ROW_FROM = ROW_FROM_HEAD + SPARE
ROW_FROM_RANK = ROW_FROM + SPARE
ROW_PARTNER = ROW_FROM_RANK + SPARE
ROW_LEFT = ROW_PARTNER + 1
ROWS = -(-(ROW_LEFT + 1) // 8) * 8


def place(chip):
    return ((chip & 3) << 4) | (chip & 12) | (chip >> 4)


def through(device, shift):
    z, x, y, c = device // 32, device // 8 % 4, device // 2 % 4, device % 2
    dz, dx, dy, dc = shift
    return (((z + dz) % 4 * 4 + (x + dx) % 4) * 4 + (y + dy) % 4) * 2 + (c ^ dc)


def shift_pairs(shift):
    return [(through(b, shift), b) for b in range(DEVICES)]


def roll_lanes(array, amount):
    amount = amount % DEVICES
    return pltpu.roll(array, amount, 1) if amount else array


def permuted(array, shift, lane, inverse=False):
    dz, dx, dy, dc = shift
    if inverse:
        dz, dx, dy = -dz % 4, -dx % 4, -dy % 4
    if dz:
        array = roll_lanes(array, -32 * dz)
    if dx:
        inside = (lane // 8) % 4 + dx < 4
        array = jnp.where(inside, roll_lanes(array, -8 * dx), roll_lanes(array, 32 - 8 * dx))
    if dy:
        inside = (lane // 2) % 4 + dy < 4
        array = jnp.where(inside, roll_lanes(array, -2 * dy), roll_lanes(array, 8 - 2 * dy))
    if dc:
        array = jnp.where(lane % 2 == 0, roll_lanes(array, -1), roll_lanes(array, 1))
    return array


def make_plan(chosen_ref, out_ref):
    chip = lax.broadcasted_iota(jnp.int32, (CHIPS, DEVICES), 0)
    lane = lax.broadcasted_iota(jnp.int32, (CHIPS, DEVICES), 1)
    even = jnp.zeros((CHIPS, DEVICES), jnp.int32)
    odd = jnp.zeros((CHIPS, DEVICES), jnp.int32)
    for entry in range(3 * HEADS):
        owner = chosen_ref[entry : entry + 1, :]
        even = even + jnp.where(owner == 2 * chip, entry // 3 + 1, 0)
        odd = odd + jnp.where(owner == 2 * chip + 1, entry // 3 + 1, 0)
    home = lane // 2 == chip
    partner = jnp.sum(jnp.where(home, even + odd, 0), axis=0, keepdims=True)
    even = jnp.where(home, 0, even)
    odd = jnp.where(home, 0, odd)
    waiting = jnp.where(even > 0, odd, 0)
    slot = jnp.where(even > 0, even - 1, jnp.where(odd > 0, odd + 15, -1))
    direct = jnp.where(even > 0, even, odd)
    free = jnp.where(home, 0, jnp.where(direct > 0, 0, 1))
    options = jnp.zeros((CHIPS, DEVICES), jnp.int32)
    for shift in sorted(set(SHIFTS)):
        options = options + permuted(free, shift, lane)
    score = options * 64 + (chip + 17 * lane) % 64
    big = 1 << 20
    out_ref[...] = jnp.zeros((ROWS, DEVICES), jnp.int32)
    for kind, shift in enumerate(SHIFTS):
        able = (waiting > 0) & (permuted(free, shift, lane) > 0)
        rated = jnp.where(able, score, big)
        best = jnp.min(rated, axis=0, keepdims=True)
        picked = able & (rated == best)
        head = jnp.sum(jnp.where(picked, waiting, 0), axis=0, keepdims=True)
        back = permuted(jnp.where(picked, waiting + 16, 0), shift, lane, inverse=True)
        waiting = jnp.where(picked, 0, waiting)
        slot = jnp.where(back > 0, back - 1, slot)
        free = jnp.where(back > 0, 0, free)
        forward = jnp.sum(jnp.where(back > 0, chip + 1, 0), axis=0, keepdims=True)
        out_ref[ROW_FORWARD + kind : ROW_FORWARD + kind + 1, :] = forward
        out_ref[ROW_FORWARD_HEAD + kind : ROW_FORWARD_HEAD + kind + 1, :] = head
    before = lax.broadcasted_iota(jnp.int32, (DEVICES, DEVICES), 0)
    after = lax.broadcasted_iota(jnp.int32, (DEVICES, DEVICES), 1)
    earlier = jnp.where((before < after) & (before % 2 == after % 2), 1.0, 0.0)
    rank = jnp.dot(
        jnp.where(waiting > 0, 1.0, 0.0), earlier, preferred_element_type=jnp.float32
    ).astype(jnp.int32)
    spare = jnp.zeros((CHIPS, DEVICES), jnp.int32)
    for index in range(SPARE):
        for core in range(2):
            chosen = (rank == index) & (lane % 2 == core)
            head = jnp.sum(jnp.where(chosen, waiting, 0), axis=1, keepdims=True)
            spare = jnp.where(lane == 2 * index + core, head, spare)
    out_ref[ROW_SPARE : ROW_SPARE + CHIPS, :] = spare
    excess = jnp.where((waiting > 0) & (rank >= SPARE), 1, 0)
    for index in range(SPARE):
        best = jnp.min(jnp.where(waiting > 0, chip, big), axis=0, keepdims=True)
        picked = (waiting > 0) & (chip == best)
        out_ref[ROW_FROM + index : ROW_FROM + index + 1, :] = jnp.where(best < big, best, 0)
        out_ref[ROW_FROM_RANK + index : ROW_FROM_RANK + index + 1, :] = jnp.minimum(
            jnp.sum(jnp.where(picked, rank, 0), axis=0, keepdims=True), SPARE - 1
        )
        out_ref[ROW_FROM_HEAD + index : ROW_FROM_HEAD + index + 1, :] = jnp.sum(
            jnp.where(picked, waiting, 0), axis=0, keepdims=True
        )
        waiting = jnp.where(picked, 0, waiting)
    excess = excess + waiting
    out_ref[ROW_PARTNER : ROW_PARTNER + 1, :] = partner
    left = jnp.max(jnp.max(excess, axis=0, keepdims=True), axis=1, keepdims=True)
    out_ref[ROW_LEFT : ROW_LEFT + 1, :] = jnp.broadcast_to(left, (1, DEVICES))
    out_ref[0:CHIPS, :] = slot
    out_ref[ROW_DIRECT : ROW_DIRECT + CHIPS, :] = direct


def columns(head):
    return pl.ds(pl.multiple_of(head * HEAD, HEAD), HEAD)


def make_table(plan, me, table):
    for entry in range(TABLE):
        table[entry] = 0

    def note(head_plus, code, wave):
        @pl.when(head_plus > 0)
        def _():
            head = head_plus - 1
            at = table[NEED + HEADS + head]
            table[head * 3 + jnp.minimum(at, 2)] = code
            table[NEED + HEADS + head] = at + 1
            table[NEED + head] = jnp.maximum(table[NEED + head], wave)

    def direct(chip, carry):
        note(plan[ROW_DIRECT + chip, me], place(chip), 0)
        return carry

    lax.fori_loop(0, CHIPS, direct, 0)
    note(plan[ROW_PARTNER, me], CODE_PARTNER, 0)
    for kind in range(KINDS):
        note(plan[ROW_FORWARD_HEAD + kind, me], CODE_FORWARD + kind, WAVE_OF[kind])
    for index in range(SPARE):
        note(plan[ROW_FROM_HEAD + index, me], CODE_SPARE + index, WAVES - 1)
    for ready in range(WAVES):

        def put(head, carry):
            @pl.when(table[NEED + head] == ready)
            def _():
                wave, so_far = ready, 0
                for earlier in range(ready):
                    so_far = so_far + table[COUNT + earlier]
                for later in range(ready, WAVES - 1):
                    so_far = so_far + table[COUNT + later]
                    full = (wave == later) & (so_far >= UP_TO[later])
                    wave = jnp.where(full, later + 1, wave)
                at = table[COUNT + wave]
                table[LIST + wave * HEADS + at] = head
                table[COUNT + wave] = at + 1

            return carry

        lax.fori_loop(0, HEADS, put, 0)


def pack_kernel(chosen, me_ref, keys_in, values_in, other_keys_in, other_values_in, *rest):
    plan_out, send, table, plan, keys, values, other_keys, other_values, sem, sems = rest
    loads = []
    pairs = zip(
        (keys_in, values_in, other_keys_in, other_values_in),
        (keys, values, other_keys, other_values),
    )
    for n, (source, into) in enumerate(pairs):
        loads.append(pltpu.make_async_copy(source, into, sems.at[n]))
        loads[-1].start()
    make_plan(chosen, plan_out)
    to_scalars = pltpu.make_async_copy(plan_out, plan, sems.at[4])
    to_scalars.start()
    to_scalars.wait()
    me = me_ref[0]
    chip, core = me >> 1, me & 1
    for load in loads:
        load.wait()

    def one_slot(dest, carry):
        code = plan[chip, 2 * dest + core]
        at = place(dest)
        cut = columns(jnp.maximum(code, 0) & 15)

        def copy(*sources):
            for half, source in enumerate(sources):
                pltpu.make_async_copy(
                    source.at[:, :, cut],
                    send.at[at >> 1, at & 1, pl.ds(half * HALF, HALF)],
                    sem,
                ).start()

        @pl.when(code >> 4 == core)
        def _():
            copy(keys, values)

        @pl.when(code >> 4 == 1 - core)
        def _():
            copy(other_keys, other_values)

        return carry + jnp.where(code >= 0, 2, 0)

    def one_spare(index, started):
        head = plan[ROW_SPARE + chip, 2 * index + core] - 1
        cut = columns(jnp.maximum(head, 0))

        def copy(*sources):
            for half, source in enumerate(sources):
                pltpu.make_async_copy(
                    source.at[:, :, cut], send.at[:, half, 2 * HALF + index], sem
                ).start()

        @pl.when((head >= 0) & (core == 1))
        def _():
            copy(keys, values)

        @pl.when((head >= 0) & (core == 0))
        def _():
            copy(other_keys, other_values)

        return started + jnp.where(head >= 0, 2, 0)

    started = lax.fori_loop(0, CHIPS, one_slot, 0)
    started = lax.fori_loop(0, SPARE, one_spare, started)
    make_table(plan, me, table)

    def wait_one(index, carry):
        pltpu.make_async_copy(
            keys.at[:, :, pl.ds(0, HEAD)], send.at[0, 0, pl.ds(0, HALF)], sem
        ).wait()
        return carry

    lax.fori_loop(0, started, wait_one, 0)


ANY = pl.BlockSpec(memory_space=pl.ANY)
SMEM = pl.BlockSpec(memory_space=pltpu.SMEM)
VMEM = pl.BlockSpec(memory_space=pltpu.VMEM)
BIG = pltpu.CompilerParams(vmem_limit_bytes=60 * 1024 * 1024)


def tiles(count):
    return jax.ShapeDtypeStruct((count, 2 * HALF, PIECE, HEAD), jnp.bfloat16)


def in_pieces(array):
    return array.reshape(HALF, PIECE, -1)


def pack(chosen_all, me, keys, values, other_keys, other_values):
    whole = pltpu.VMEM((HALF, PIECE, HEADS * HEAD), jnp.bfloat16)
    return pl.pallas_call(
        pack_kernel,
        in_specs=[VMEM, SMEM, ANY, ANY, ANY, ANY],
        out_specs=[VMEM, ANY, SMEM],
        out_shape=[
            jax.ShapeDtypeStruct((ROWS, DEVICES), jnp.int32),
            jax.ShapeDtypeStruct((HALF, 2, SLOT_PIECES, PIECE, HEAD), jnp.bfloat16),
            jax.ShapeDtypeStruct((TABLE,), jnp.int32),
        ],
        scratch_shapes=[pltpu.SMEM((ROWS, DEVICES), jnp.int32)]
        + [whole] * 4
        + [pltpu.SemaphoreType.DMA, pltpu.SemaphoreType.DMA((5,))],
        compiler_params=BIG,
        name="pack",
    )(chosen_all, me, *map(in_pieces, (keys, values, other_keys, other_values)))


def forward_kernel(plan, me_ref, arrived, *rest):
    outs, (moving, spare, gathered, sems, out_sems) = rest[:-5], rest[-5:]
    me = me_ref[0]
    core = me & 1
    load_spare = pltpu.make_async_copy(
        arrived.at[:, pl.ds(2 * HALF, SPARE)], spare, sems.at[KINDS]
    )
    load_spare.start()
    steps = []
    for kind in range(KINDS):
        out = outs[1].at[kind] if kind < PARTNER else outs[kind - PARTNER + 2].at[0]
        chip = plan[ROW_FORWARD + kind, me] - 1
        source = arrived.at[place(jnp.maximum(chip, 0)), pl.ds(0, 2 * HALF)]
        load = pltpu.make_async_copy(source, moving.at[kind], sems.at[kind])
        store = pltpu.make_async_copy(moving.at[kind], out, out_sems.at[kind])
        steps.append((chip >= 0, load, store))
    for used, load, _ in steps:

        @pl.when(used)
        def _():
            load.start()

    load_spare.wait()

    def one_dest(dest, carry):
        device = 2 * dest + core

        def move(index):
            @pl.when(plan[ROW_FROM_HEAD + index, device] > 0)
            def _():
                chip = plan[ROW_FROM + index, device]
                rank = plan[ROW_FROM_RANK + index, device]
                gathered[place(dest), index] = spare[place(chip), rank]
                if index + 1 < SPARE:
                    move(index + 1)

        move(0)
        return carry

    lax.fori_loop(0, CHIPS, one_dest, 0)
    last = pltpu.make_async_copy(gathered, outs[0], out_sems.at[KINDS])
    last.start()
    for used, load, store in steps:

        @pl.when(used)
        def _():
            load.wait()
            store.start()

    for used, _, store in steps:

        @pl.when(used)
        def _():
            store.wait()

    last.wait()


def forward(plan, me, arrived):
    return pl.pallas_call(
        forward_kernel,
        in_specs=[SMEM, SMEM, ANY],
        out_specs=[ANY] * (KINDS - PARTNER + 2),
        out_shape=[jax.ShapeDtypeStruct((CHIPS, SPARE, PIECE, HEAD), jnp.bfloat16)]
        + [tiles(PARTNER)]
        + [tiles(1)] * (KINDS - PARTNER),
        scratch_shapes=[
            pltpu.VMEM((KINDS, 2 * HALF, PIECE, HEAD), jnp.bfloat16),
            pltpu.VMEM((CHIPS, SPARE, PIECE, HEAD), jnp.bfloat16),
            pltpu.VMEM((CHIPS, SPARE, PIECE, HEAD), jnp.bfloat16),
            pltpu.SemaphoreType.DMA((KINDS + 1,)),
            pltpu.SemaphoreType.DMA((KINDS + 1,)),
        ],
        compiler_params=BIG,
        name="forward",
    )(plan, me, arrived)


ROWS_AT_ONCE = 256


def scores_of(query, key):
    return lax.dot_general(
        query, key, (((1,), (1,)), ((), ())), preferred_element_type=jnp.float32
    )


def attend_kernel(wave, kinds, table, queries, keys, values, *rest):
    other_keys, other_values, arrived = rest[:3]
    forwarded = dict(zip(kinds, rest[3 : 3 + len(kinds)]))
    pieces = rest[3 + len(kinds)] if wave == WAVES - 1 else None
    out, query_buf, key_buf, value_buf, out_buf, sems, out_sems = rest[-7:]
    count = table[COUNT + wave]

    def head_at(index):
        return table[LIST + wave * HEADS + index]

    def load(index, slot):
        head = head_at(index)

        def start(j, source_key, source_value):
            into_value = value_buf.at[slot, j, :, :, pl.ds(0, HEAD)]
            pltpu.make_async_copy(source_key, key_buf.at[slot, j], sems.at[slot, 2 * j]).start()
            pltpu.make_async_copy(source_value, into_value, sems.at[slot, 2 * j + 1]).start()

        cut = columns(head)
        pltpu.make_async_copy(queries.at[:, :, cut], query_buf.at[slot], sems.at[slot, 8]).start()
        start(3, keys.at[:, :, cut], values.at[:, :, cut])
        for j in range(3):
            code = table[head * 3 + j]

            @pl.when(code < CHIPS)
            def _():
                start(j, arrived.at[code, pl.ds(0, HALF)], arrived.at[code, pl.ds(HALF, HALF)])

            @pl.when(code >= CHIPS)
            def _():
                @pl.when(code == CODE_PARTNER)
                def _():
                    start(j, other_keys.at[:, :, cut], other_values.at[:, :, cut])

                for kind, ref in forwarded.items():
                    last = kind + (PARTNER if kind == 0 else 1)

                    @pl.when((code >= CODE_FORWARD + kind) & (code < CODE_FORWARD + last))
                    def _():
                        tile = ref.at[code - CODE_FORWARD - kind]
                        start(j, tile.at[pl.ds(0, HALF)], tile.at[pl.ds(HALF, HALF)])

                if pieces is not None:

                    @pl.when(code >= CODE_SPARE)
                    def _():
                        start(j, pieces.at[:, 0, code - CODE_SPARE], pieces.at[:, 1, code - CODE_SPARE])

    def store(index, slot):
        return pltpu.make_async_copy(
            out_buf.at[slot], out.at[:, :, columns(head_at(index))], out_sems.at[slot]
        )

    @pl.when(count > 0)
    def _():
        load(0, 0)
        ones = jnp.ones((HALF, PIECE, HEAD), jnp.bfloat16)
        for slot in range(2):
            for j in range(4):
                value_buf[slot, j, :, :, HEAD:] = ones

    def one_head(index, carry):
        slot = index % 2

        @pl.when(index + 1 < count)
        def _():
            load(index + 1, 1 - slot)

        for j in range(4):
            into_value = value_buf.at[slot, j, :, :, pl.ds(0, HEAD)]
            tile = arrived.at[0, pl.ds(0, HALF)]
            pltpu.make_async_copy(tile, key_buf.at[slot, j], sems.at[slot, 2 * j]).wait()
            pltpu.make_async_copy(tile, into_value, sems.at[slot, 2 * j + 1]).wait()
        pltpu.make_async_copy(tile, query_buf.at[slot], sems.at[slot, 8]).wait()

        @pl.when(index >= 2)
        def _():
            store(index - 2, slot).wait()

        query = query_buf[slot].reshape(BLOCK, HEAD)
        for start in range(0, BLOCK, ROWS_AT_ONCE):
            stop = start + ROWS_AT_ONCE
            q = query[start:stop, :]
            total = highest = None
            for j in (3, 0, 1, 2):
                seen = stop if j == 3 else BLOCK
                scores = scores_of(q, key_buf[slot, j, 0 : seen // PIECE].reshape(seen, HEAD))
                if j == 3:
                    row_iota = lax.broadcasted_iota(jnp.int32, scores.shape, 0) + start
                    col_iota = lax.broadcasted_iota(jnp.int32, scores.shape, 1)
                    scores = jnp.where(col_iota <= row_iota, scores, -jnp.inf)
                top = jnp.max(scores, axis=1, keepdims=True)
                if highest is not None:
                    top = jnp.maximum(highest, top)
                weight = jnp.exp2((scores - top) * SCALE).astype(jnp.bfloat16)
                value = value_buf[slot, j, 0 : seen // PIECE].reshape(seen, 2 * HEAD)
                added = jnp.dot(weight, value, preferred_element_type=jnp.float32)
                if highest is None:
                    total = added
                else:
                    total = total * jnp.exp2((highest - top) * SCALE) + added
                highest = top
            result = (total[:, :HEAD] / total[:, HEAD:]).astype(jnp.bfloat16)
            span = slice(start // PIECE, stop // PIECE)
            out_buf[slot, span] = result.reshape(ROWS_AT_ONCE // PIECE, PIECE, HEAD)
        store(index, slot).start()
        return carry

    lax.fori_loop(0, count, one_head, 0)

    @pl.when(count >= 2)
    def _():
        store(count - 2, count % 2).wait()

    @pl.when(count >= 1)
    def _():
        store(count - 1, (count - 1) % 2).wait()


HEADS_EXPECTED = (9, 4, 2, 2)


def attend(wave, before, table, queries, keys, values, others, arrived, forwarded, pieces):
    kinds = [kind for kind in forwarded if WAVE_OF[kind] <= wave]
    operands = [table, *map(in_pieces, (queries, keys, values, *others)), arrived]
    operands += [forwarded[kind] for kind in kinds]
    if wave == WAVES - 1:
        operands.append(pieces.reshape(HALF, 2, SPARE, PIECE, HEAD))
    if before is not None:
        operands.append(before)
    size = HEADS_EXPECTED[wave] * BLOCK * 4 * BLOCK * HEAD
    return pl.pallas_call(
        lambda *refs: attend_kernel(wave, kinds, *refs),
        in_specs=[SMEM] + [ANY] * (len(operands) - 1),
        out_specs=ANY,
        out_shape=jax.ShapeDtypeStruct((HALF, PIECE, HEADS * HEAD), jnp.bfloat16),
        input_output_aliases={} if before is None else {len(operands) - 1: 0},
        scratch_shapes=[
            pltpu.VMEM((2, HALF, PIECE, HEAD), jnp.bfloat16),
            pltpu.VMEM((2, 4, HALF, PIECE, HEAD), jnp.bfloat16),
            pltpu.VMEM((2, 4, HALF, PIECE, 2 * HEAD), jnp.bfloat16),
            pltpu.VMEM((2, HALF, PIECE, HEAD), jnp.bfloat16),
            pltpu.SemaphoreType.DMA((2, 9)),
            pltpu.SemaphoreType.DMA((2,)),
        ],
        cost_estimate=pl.CostEstimate(
            flops=16 * size, bytes_accessed=3 * 2**20, transcendentals=size // HEAD
        ),
        compiler_params=BIG,
        name="attend",
    )(*operands)


LANES = [[2 * place(at) + core for at in range(CHIPS)] for core in range(2)]
SWAP = [(device, device ^ 1) for device in range(DEVICES)]


def exchange(array):
    return lax.all_to_all(array, "ctx", 0, 0, axis_index_groups=LANES, tiled=True)


def full_attention(queries, keys, values, chosen_all, me):
    heads = jnp.arange(3 * HEADS, dtype=jnp.int32) // 3
    mine = lax.dynamic_index_in_dim(chosen_all, me, 0, keepdims=False)
    wants = chosen_all == me
    which = jnp.max(jnp.where(wants, heads[None, :], 0), axis=1)
    key_heads = keys.reshape(BLOCK, HEADS, HEAD).transpose(1, 0, 2)
    value_heads = values.reshape(BLOCK, HEADS, HEAD).transpose(1, 0, 2)
    got_key = lax.all_to_all(jnp.take(key_heads, which, axis=0), "ctx", 0, 0, tiled=True)
    got_value = lax.all_to_all(jnp.take(value_heads, which, axis=0), "ctx", 0, 0, tiled=True)
    q_heads = queries.reshape(BLOCK, HEADS, HEAD).transpose(1, 0, 2)
    allowed = jnp.arange(4 * BLOCK)[None, :] >= BLOCK
    allowed = allowed | (jnp.arange(4 * BLOCK)[None, :] <= jnp.arange(BLOCK)[:, None])

    def one_head(head):
        picks = lax.dynamic_slice(mine, (3 * head,), (3,))
        k = jnp.concatenate([key_heads[head], got_key[picks].reshape(3 * BLOCK, HEAD)], axis=0)
        v = jnp.concatenate([value_heads[head], got_value[picks].reshape(3 * BLOCK, HEAD)], axis=0)
        s = jnp.where(allowed, scores_of(q_heads[head], k), -jnp.inf)
        weight = jnp.exp2((s - jnp.max(s, axis=1, keepdims=True)) * SCALE)
        total = jnp.sum(weight, axis=1, keepdims=True)
        o = jnp.dot(weight.astype(jnp.bfloat16), v, preferred_element_type=jnp.float32)
        return (o / total).astype(jnp.bfloat16)

    out = lax.map(one_head, jnp.arange(HEADS))
    return out.transpose(1, 0, 2).reshape(BLOCK, HEADS * HEAD)


def body(queries, keys, values, chosen):
    me = lax.axis_index("ctx").astype(jnp.int32)
    me_ref = me.reshape(1)
    other_keys = lax.ppermute(keys, "ctx", SWAP)
    other_values = lax.ppermute(values, "ctx", SWAP)
    spread = jnp.broadcast_to(chosen.reshape(1, 3 * HEADS), (DEVICES, 3 * HEADS))
    chosen_all = lax.all_to_all(spread, "ctx", 0, 0, tiled=True)
    plan, send, table = pack(chosen_all.T, me_ref, keys, values, other_keys, other_values)
    sent = exchange(send.reshape(CHIPS, SLOT_ROWS, HEAD))
    held = (sent, plan, table, queries, keys, values, other_keys, other_values, me_ref)
    held = lax.optimization_barrier(held)
    arrived, plan, table, queries, keys, values, other_keys, other_values, me_ref = held
    arrived = arrived.reshape(CHIPS, SLOT_PIECES, PIECE, HEAD)
    pieces, *outgoing = forward(plan, me_ref, arrived)
    pieces = exchange(pieces)
    outgoing = dict(zip([0, *range(PARTNER, KINDS)], outgoing))
    forwarded = {}
    out = None
    for wave in range(WAVES):
        if wave:
            for kind in [kind for kind in outgoing if WAVE_OF[kind] == wave]:
                forwarded[kind] = lax.ppermute(outgoing[kind], "ctx", shift_pairs(SHIFTS[kind]))
        out = attend(
            wave,
            out,
            table,
            queries,
            keys,
            values,
            (other_keys, other_values),
            arrived,
            forwarded,
            pieces,
        )
    out = out.reshape(BLOCK, HEADS * HEAD)
    return lax.cond(
        plan[ROW_LEFT, 0] > 0,
        lambda: full_attention(queries, keys, values, chosen_all, me),
        lambda: out,
    )


def solution(mesh):
    placed = (P("ctx", None), P("ctx", None), P("ctx", None), P("ctx", None, None))
    return jax.shard_map(
        body, mesh=mesh, in_specs=placed, out_specs=P("ctx", None), check_vma=False
    )
```

profile of v0, /device:TPU:7, one launch (start us, length us, event | category | flops | bytes accessed | tf_op | source)
XLA Modules:
  0.0 328.2 jit_solution(15172817319053426677)
XLA Ops:
  0.0 0.7 collective-permute-start
  0.7 0.0 collective-permute-start.1
  0.7 0.8 copy.30
  1.4 0.1 broadcast_in_dim.55
  1.5 0.7 broadcast_in_dim.56
  2.2 10.6 %all-to-all-start.2 = ((s32[128,1,48]{2,1,0:T(1,128)}), s32[128,1,48]{2,1,0:T(1,128)S(1)}, u32[]{:S(2)}, u32[]{:S(2)}) async-start(s32[128,1,48]{2,1,0:T(1,128)} %broadcast_in_dim.56), calls=%async_computation.2 | async-start | bytes 131072 | tf_op jit(solution)/shard_map/all_to_all | solution.py:592
  12.8 7.9 %all-to-all-done.2 = s32[128,1,48]{2,1,0:T(1,128)S(1)} async-done(((s32[128,1,48]{2,1,0:T(1,128)}), s32[128,1,48]{2,1,0:T(1,128)S(1)}, u32[]{:S(2)}, u32[]{:S(2)}) %all-to-all-start.2) | async-done | bytes 24608 | tf_op jit(solution)/shard_map/all_to_all | solution.py:592
  20.7 0.1 copy.31
  20.8 0.0 collective-permute-done
  20.8 0.0 copy-start.3
  20.8 0.0 collective-permute-done.1
  20.8 1.3 copy-done.3
  22.1 13.4 %pack.1 = (s32[248,128]{1,0:T(8,128)}, bf16[32,2,69,16,128]{4,3,2,1,0:T(8,128)(2,1)}, s32[148]{0:T(256)}) custom-call(s32[48,128]{1,0:T(8,128)S(1)} %bitcast.100, s32[1]{0:T(128)} %bitcast.13.me_ref, bf16[32,16,2048]{2,1,0:T(8,128)(2,1)} %bitcast.73, bf16[32,16,2048]{2,1,0:T(8,128)(2,1)} %bitcast.78, bf16[32,16,2048]{2,1,0:T(8,128)(2,1)} %bitcast.83, ...), custom_call_target="tpu_custom_call" | custom-call | tf_op jit(solution)/shard_map/pack/pallas_call | solution.py:294
  35.6 205.3 %all_to_all.28 = bf16[64,1104,128]{2,1,0:T(8,128)(2,1)} all-to-all(bf16[64,1104,128]{2,1,0:T(8,128)(2,1)} %bitcast.93), channel_id=1, replica_groups={{0,32,64,96,8,40,72,104,16,48,80,112,24,56,88,120,2,34,66,98,10,42,74,1..., dimensions={0} | all-to-all | bytes 36175872 | tf_op jit(solution)/shard_map/all_to_all | solution.py:556
  240.9 0.0 copy-start.1
  240.9 6.9 %forward.1 = (bf16[64,5,16,128]{3,2,1,0:T(8,128)(2,1)}, bf16[6,64,16,128]{3,2,1,0:T(8,128)(2,1)}, bf16[1,64,16,128]{3,2,1,0:T(8,128)(2,1)}, bf16[1,64,16,128]{3,...) custom-call(s32[248,128]{1,0:T(8,128)} %get-tuple-element.181.plan, ...), custom_call_target="tpu_custom_call" | custom-call | tf_op jit(solution)/shard_map/forward/pallas_call | solution.py:370
  247.8 2.7 collective-permute-start.2
  250.6 0.5 collective-permute-start.3
  251.1 1.3 collective-permute-start.4
  252.4 0.4 collective-permute-start.5
  252.8 1.3 collective-permute-start.6
  254.1 13.7 %all-to-all-start.4 = ((bf16[64,5,16,128]{3,2,1,0:T(8,128)(2,1)}), bf16[64,5,16,128]{3,2,1,0:T(8,128)(2,1)S(1)}, u32[]{:S(2)}, u32[]{:S(2)}) async-start(bf16[64,5,16,128]{3,2,1,0:T(8,128)(2,1)} %get-tuple-element.203), calls=%async_computation.4 | async-start | bytes 2621440 | tf_op jit(solution)/shard_map/all_to_all | solution.py:556
  267.8 0.0 copy-done.1
  267.8 15.1 %attend.4.refs_12_ = bf16[32,16,2048]{2,1,0:T(8,128)(2,1)} custom-call(s32[148]{0:T(256)} %get-tuple-element.182.refs_0_, bf16[32,16,2048]{2,1,0:T(8,128)(2,1)} %bitcast.88, bf16[32,16,2048]{2,1,0:T(8,128)(2,1)S(1)} %bitcast.74, bf16[32,16,2048]{2,1,0:T(8,128)(2,1)} %bitcast.79, bf16[32,16,2048]{2,1,0:T(8,128)(2,1)} %bitcast.84, ...), custom_call_target="tpu_custom_call" | custom-call | flops 19327352832 | bytes 3145728 | tf_op jit(solution)/shard_map/attend/pallas_call | solution.py:529
  282.9 1.2 slice.3
  284.7 0.0 collective-permute-done.3.refs_8_
  284.7 2.5 collective-permute-start.10
  287.2 0.0 collective-permute-done.4.refs_9_
  287.2 1.3 collective-permute-start.7
  288.5 0.0 collective-permute-done.5.refs_10_
  288.5 0.6 collective-permute-start.8
  289.2 0.0 collective-permute-done.6.refs_11_
  289.2 1.5 collective-permute-start.9
  290.7 0.0 collective-permute-done.2.refs_7_
  290.7 3.2 collective-permute-start.11
  294.0 11.9 %attend.5.refs_16_ = bf16[32,16,2048]{2,1,0:T(8,128)(2,1)} custom-call(s32[148]{0:T(256)} %get-tuple-element.182.refs_0_, bf16[32,16,2048]{2,1,0:T(8,128)(2,1)} %bitcast.89, bf16[32,16,2048]{2,1,0:T(8,128)(2,1)S(1)} %bitcast.75, bf16[32,16,2048]{2,1,0:T(8,128)(2,1)} %bitcast.80, bf16[32,16,2048]{2,1,0:T(8,128)(2,1)} %bitcast.85, ...), custom_call_target="tpu_custom_call", output_to_operand_aliasing={{}: (12, {})} | custom-call | flops 8589934592 | bytes 3145728 | tf_op jit(solution)/shard_map/attend/pallas_call | solution.py:529
  305.9 0.0 collective-permute-done.10.refs_15_
  305.9 0.0 copy-start.5
  305.9 0.1 collective-permute-start.12
  306.0 0.0 collective-permute-done.7.refs_12_
  306.0 0.0 copy-start.6
  306.0 0.4 collective-permute-start.13
  306.4 0.0 collective-permute-done.8.refs_13_
  306.4 1.4 collective-permute-start.14
  307.8 0.0 collective-permute-done.9.refs_14_
  307.8 0.0 copy-done.5
  307.8 0.0 copy-done.6
  307.8 6.3 %attend.6.refs_21_ = bf16[32,16,2048]{2,1,0:T(8,128)(2,1)} custom-call(s32[148]{0:T(256)} %get-tuple-element.182.refs_0_, bf16[32,16,2048]{2,1,0:T(8,128)(2,1)} %bitcast.90, bf16[32,16,2048]{2,1,0:T(8,128)(2,1)S(1)} %bitcast.76, bf16[32,16,2048]{2,1,0:T(8,128)(2,1)} %bitcast.81, bf16[32,16,2048]{2,1,0:T(8,128)(2,1)} %bitcast.86, ...), custom_call_target="tpu_custom_call", output_to_operand_aliasing={{}: (16, {})} | custom-call | flops 4294967296 | bytes 3145728 | tf_op jit(solution)/shard_map/attend/pallas_call | solution.py:529
  314.1 0.0 collective-permute-done.11.refs_16_
  314.1 0.0 collective-permute-done.12.refs_17_
  314.1 1.4 collective-permute-done.13.refs_18_
  315.5 5.1 %collective-permute-done.14.refs_19_ = bf16[1,64,16,128]{3,2,1,0:T(8,128)(2,1)} collective-permute-done((bf16[1,64,16,128]{3,2,1,0:T(8,128)(2,1)}, bf16[1,64,16,128]{3,2,1,0:T(8,128)(2,1)}, u32[]{:S(2)}, u32[]{:S(2)}) %collective-permute-start.14) | collective-permute-done | bytes 262176 | tf_op jit(solution)/shard_map/ppermute | solution.py:607
  320.7 0.0 all-to-all-done.4
  320.7 0.0 copy-start.4
  320.7 1.1 copy-done.4
  321.8 6.2 %attend.7 = bf16[32,16,2048]{2,1,0:T(8,128)(2,1)} custom-call(s32[148]{0:T(256)} %get-tuple-element.182.refs_0_, bf16[32,16,2048]{2,1,0:T(8,128)(2,1)} %bitcast.91, bf16[32,16,2048]{2,1,0:T(8,128)(2,1)S(1)} %bitcast.77, bf16[32,16,2048]{2,1,0:T(8,128)(2,1)} %bitcast.82, bf16[32,16,2048]{2,1,0:T(8,128)(2,1)} %bitcast.87, ...), custom_call_target="tpu_custom_call", output_to_operand_aliasing={{}: (21, {})} | custom-call | flops 4294967296 | bytes 3145728 | tf_op jit(solution)/shard_map/attend/pallas_call | solution.py:529
  (1 shorter events, 0.0 us)
Async XLA Ops:
  0.0 20.8 %collective-permute-start = (bf16[512,2048]{1,0:T(8,128)(2,1)}, bf16[512,2048]{1,0:T(8,128)(2,1)S(1)}, u32[]{:S(2)}, u32[]{:S(2)}) collective-permute-start(bf16[512,2048]{1,0:T(8,128)(2,1)} %param.11), channel_id=1, source_target_pairs={{0,1},{1,0},{2,3},{3,2},{4,5},{5,4},{6,7},{7,6},{8,9},{9,8},{10,11... | collective-permute-start | bytes 6291464 | tf_op jit(solution)/shard_map/ppermute | solution.py:589
  0.7 20.1 %collective-permute-start.1 = (bf16[512,2048]{1,0:T(8,128)(2,1)}, bf16[512,2048]{1,0:T(8,128)(2,1)}, u32[]{:S(2)}, u32[]{:S(2)}) collective-permute-start(bf16[512,2048]{1,0:T(8,128)(2,1)} %param.12), channel_id=1, source_target_pairs={{0,1},{1,0},{2,3},{3,2},{4,5},{5,4},{6,7},{7,6},{8,9},{9,8},{10,11... | collective-permute-start | bytes 6291464 | tf_op jit(solution)/shard_map/ppermute | solution.py:590
  2.2 18.5 %all-to-all-start.2 = ((s32[128,1,48]{2,1,0:T(1,128)}), s32[128,1,48]{2,1,0:T(1,128)S(1)}, u32[]{:S(2)}, u32[]{:S(2)}) async-start(s32[128,1,48]{2,1,0:T(1,128)} %broadcast_in_dim.56), calls=%async_computation.2 | async-start | bytes 131072 | tf_op jit(solution)/shard_map/all_to_all | solution.py:592
  20.8 1.3 copy-start.3
  240.9 26.9 %copy-start.1 = (bf16[512,2048]{1,0:T(8,128)(2,1)S(1)}, bf16[512,2048]{1,0:T(8,128)(2,1)}, u32[]{:S(2)}) copy-start(bf16[512,2048]{1,0:T(8,128)(2,1)} %param.11) | copy-start | bytes 6291460
  247.8 42.9 %collective-permute-start.2 = (bf16[6,64,16,128]{3,2,1,0:T(8,128)(2,1)}, bf16[6,64,16,128]{3,2,1,0:T(8,128)(2,1)}, u32[]{:S(2)}, u32[]{:S(2)}) collective-permute-start(bf16[6,64,16,128]{3,2,1,0:T(8,128)(2,1)} %get-tuple-element.190), channel_id=1, source_target_pairs={{1,0},{0,1},{3,2},{2,3},{5,4},{4,5},{7,6},{6,7},{9,8},{8,9},{11,10... | collective-permute-start | bytes 4718600 | tf_op jit(solution)/shard_map/ppermute | solution.py:607
  250.6 34.1 %collective-permute-start.3 = (bf16[1,64,16,128]{3,2,1,0:T(8,128)(2,1)}, bf16[1,64,16,128]{3,2,1,0:T(8,128)(2,1)}, u32[]{:S(2)}, u32[]{:S(2)}) collective-permute-start(bf16[1,64,16,128]{3,2,1,0:T(8,128)(2,1)} %get-tuple-element.191), channel_id=1, source_target_pairs={{32,0},{33,1},{34,2},{35,3},{36,4},{37,5},{38,6},{39,7},{40,8},{41... | collective-permute-start | bytes 786440 | tf_op jit(solution)/shard_map/ppermute | solution.py:607
  251.1 36.1 %collective-permute-start.4 = (bf16[1,64,16,128]{3,2,1,0:T(8,128)(2,1)}, bf16[1,64,16,128]{3,2,1,0:T(8,128)(2,1)}, u32[]{:S(2)}, u32[]{:S(2)}) collective-permute-start(bf16[1,64,16,128]{3,2,1,0:T(8,128)(2,1)} %get-tuple-element.192), channel_id=1, source_target_pairs={{33,0},{32,1},{35,2},{34,3},{37,4},{36,5},{39,6},{38,7},{41,8},{40... | collective-permute-start | bytes 786440 | tf_op jit(solution)/shard_map/ppermute | solution.py:607
  252.4 36.1 %collective-permute-start.5 = (bf16[1,64,16,128]{3,2,1,0:T(8,128)(2,1)}, bf16[1,64,16,128]{3,2,1,0:T(8,128)(2,1)}, u32[]{:S(2)}, u32[]{:S(2)}) collective-permute-start(bf16[1,64,16,128]{3,2,1,0:T(8,128)(2,1)} %get-tuple-element.193), channel_id=1, source_target_pairs={{96,0},{97,1},{98,2},{99,3},{100,4},{101,5},{102,6},{103,7},{104,8... | collective-permute-start | bytes 786440 | tf_op jit(solution)/shard_map/ppermute | solution.py:607
  252.8 36.4 %collective-permute-start.6 = (bf16[1,64,16,128]{3,2,1,0:T(8,128)(2,1)}, bf16[1,64,16,128]{3,2,1,0:T(8,128)(2,1)}, u32[]{:S(2)}, u32[]{:S(2)}) collective-permute-start(bf16[1,64,16,128]{3,2,1,0:T(8,128)(2,1)} %get-tuple-element.194), channel_id=1, source_target_pairs={{97,0},{96,1},{99,2},{98,3},{101,4},{100,5},{103,6},{102,7},{105,8... | collective-permute-start | bytes 786440 | tf_op jit(solution)/shard_map/ppermute | solution.py:607
  254.1 66.6 %all-to-all-start.4 = ((bf16[64,5,16,128]{3,2,1,0:T(8,128)(2,1)}), bf16[64,5,16,128]{3,2,1,0:T(8,128)(2,1)S(1)}, u32[]{:S(2)}, u32[]{:S(2)}) async-start(bf16[64,5,16,128]{3,2,1,0:T(8,128)(2,1)} %get-tuple-element.203), calls=%async_computation.4 | async-start | bytes 2621440 | tf_op jit(solution)/shard_map/all_to_all | solution.py:556
  284.7 21.2 %collective-permute-start.10 = (bf16[1,64,16,128]{3,2,1,0:T(8,128)(2,1)}, bf16[1,64,16,128]{3,2,1,0:T(8,128)(2,1)S(1)}, u32[]{:S(2)}, u32[]{:S(2)}) collective-permute-start(bf16[1,64,16,128]{3,2,1,0:T(8,128)(2,1)} %get-tuple-element.198), channel_id=1, source_target_pairs={{25,0},{24,1},{27,2},{26,3},{29,4},{28,5},{31,6},{30,7},{1,8},{0,9... | collective-permute-start | bytes 786440 | tf_op jit(solution)/shard_map/ppermute | solution.py:607
  287.2 18.7 %collective-permute-start.7 = (bf16[1,64,16,128]{3,2,1,0:T(8,128)(2,1)}, bf16[1,64,16,128]{3,2,1,0:T(8,128)(2,1)S(1)}, u32[]{:S(2)}, u32[]{:S(2)}) collective-permute-start(bf16[1,64,16,128]{3,2,1,0:T(8,128)(2,1)} %get-tuple-element.195), channel_id=1, source_target_pairs={{8,0},{9,1},{10,2},{11,3},{12,4},{13,5},{14,6},{15,7},{16,8},{17,9... | collective-permute-start | bytes 786440 | tf_op jit(solution)/shard_map/ppermute | solution.py:607
  288.5 17.9 %collective-permute-start.8 = (bf16[1,64,16,128]{3,2,1,0:T(8,128)(2,1)}, bf16[1,64,16,128]{3,2,1,0:T(8,128)(2,1)}, u32[]{:S(2)}, u32[]{:S(2)}) collective-permute-start(bf16[1,64,16,128]{3,2,1,0:T(8,128)(2,1)} %get-tuple-element.196), channel_id=1, source_target_pairs={{9,0},{8,1},{11,2},{10,3},{13,4},{12,5},{15,6},{14,7},{17,8},{16,9... | collective-permute-start | bytes 786440 | tf_op jit(solution)/shard_map/ppermute | solution.py:607
  289.2 18.6 %collective-permute-start.9 = (bf16[1,64,16,128]{3,2,1,0:T(8,128)(2,1)}, bf16[1,64,16,128]{3,2,1,0:T(8,128)(2,1)}, u32[]{:S(2)}, u32[]{:S(2)}) collective-permute-start(bf16[1,64,16,128]{3,2,1,0:T(8,128)(2,1)} %get-tuple-element.197), channel_id=1, source_target_pairs={{24,0},{25,1},{26,2},{27,3},{28,4},{29,5},{30,6},{31,7},{0,8},{1,9... | collective-permute-start | bytes 786440 | tf_op jit(solution)/shard_map/ppermute | solution.py:607
  290.7 23.4 %collective-permute-start.11 = (bf16[1,64,16,128]{3,2,1,0:T(8,128)(2,1)}, bf16[1,64,16,128]{3,2,1,0:T(8,128)(2,1)}, u32[]{:S(2)}, u32[]{:S(2)}) collective-permute-start(bf16[1,64,16,128]{3,2,1,0:T(8,128)(2,1)} %get-tuple-element.199), channel_id=1, source_target_pairs={{2,0},{3,1},{4,2},{5,3},{6,4},{7,5},{0,6},{1,7},{10,8},{11,9},{12,... | collective-permute-start | bytes 786440 | tf_op jit(solution)/shard_map/ppermute | solution.py:607
  305.9 1.9 copy-start.5
  305.9 8.2 %collective-permute-start.12 = (bf16[1,64,16,128]{3,2,1,0:T(8,128)(2,1)}, bf16[1,64,16,128]{3,2,1,0:T(8,128)(2,1)}, u32[]{:S(2)}, u32[]{:S(2)}) collective-permute-start(bf16[1,64,16,128]{3,2,1,0:T(8,128)(2,1)} %get-tuple-element.200), channel_id=1, source_target_pairs={{3,0},{2,1},{5,2},{4,3},{7,4},{6,5},{1,6},{0,7},{11,8},{10,9},{13,... | collective-permute-start | bytes 786440 | tf_op jit(solution)/shard_map/ppermute | solution.py:607
  306.0 1.8 copy-start.6
  306.0 9.5 %collective-permute-start.13 = (bf16[1,64,16,128]{3,2,1,0:T(8,128)(2,1)}, bf16[1,64,16,128]{3,2,1,0:T(8,128)(2,1)}, u32[]{:S(2)}, u32[]{:S(2)}) collective-permute-start(bf16[1,64,16,128]{3,2,1,0:T(8,128)(2,1)} %get-tuple-element.201), channel_id=1, source_target_pairs={{6,0},{7,1},{0,2},{1,3},{2,4},{3,5},{4,6},{5,7},{14,8},{15,9},{8,1... | collective-permute-start | bytes 786440 | tf_op jit(solution)/shard_map/ppermute | solution.py:607
  306.4 14.3 %collective-permute-start.14 = (bf16[1,64,16,128]{3,2,1,0:T(8,128)(2,1)}, bf16[1,64,16,128]{3,2,1,0:T(8,128)(2,1)}, u32[]{:S(2)}, u32[]{:S(2)}) collective-permute-start(bf16[1,64,16,128]{3,2,1,0:T(8,128)(2,1)} %get-tuple-element.202), channel_id=1, source_target_pairs={{7,0},{6,1},{1,2},{0,3},{3,4},{2,5},{5,6},{4,7},{15,8},{14,9},{9,1... | collective-permute-start | bytes 786440 | tf_op jit(solution)/shard_map/ppermute | solution.py:607
  320.7 1.1 copy-start.4
where the time goes:
time: 328 us
  blocking collectives  205 us (62%)
  Pallas kernels  59.9 us (18%)
  starting transfers between devices  42.3 us (13%)
  waiting for transfers between devices  14.5 us (4%)
  local copies, waits for them, and re-layouts  5.16 us (2%)
    all_to_all x1, blocking collectives, exchange(): lax.all_to_all(array, 'ctx', 0, 0, axis_index_groups=LANES, tiled=True)  205 us
    pallas_call x4, Pallas kernels, attend(): pl.pallas_call(lambda *refs: attend_kernel(wave, kinds, *refs), in_specs=...  39.5 us
    ppermute x13, starting transfers between devices, body(): lax.ppermute(outgoing[kind], 'ctx', shift_pairs(SHIFTS[kind]))  17.4 us
    all_to_all x1, starting transfers between devices, exchange(): lax.all_to_all(array, 'ctx', 0, 0, axis_index_groups=LANES, tiled=True)  13.7 us
    pallas_call x1, Pallas kernels, pack(): pl.pallas_call(pack_kernel, in_specs=[VMEM, SMEM, ANY, ANY, ANY, ANY], ou...  13.4 us
    all_to_all x1, starting transfers between devices, body(): chosen_all = lax.all_to_all(spread, 'ctx', 0, 0, tiled=True)  10.6 us
    all_to_all x1, waiting for transfers between devices, body(): chosen_all = lax.all_to_all(spread, 'ctx', 0, 0, tiled=True)  7.87 us
    pallas_call x1, Pallas kernels, forward(): pl.pallas_call(forward_kernel, in_specs=[SMEM, SMEM, ANY], out_specs=[ANY...  6.94 us
  transfers between devices with their start and end apart: 17, of which 3 were waited for; matrix products, arithmetic and copies ran while one was open for 1% of the time, Pallas kernels for 10%

commit v1 on v0

--- a/solution.py
+++ b/solution.py
@@ -22,7 +22,7 @@
 SPARE = 5
 PIECE = 16
 WAVES = 4
-UP_TO = (8, 12, 15)
+UP_TO = (8, 12, 16)
 WAVE_OF = [1] * (PARTNER + 4) + [2] * 4 + [3] * 4
 CODE_PARTNER = CHIPS
 CODE_FORWARD = CODE_PARTNER + 1

time: 328 us -> 326 us (level); the launches traced: 328 us -> 322 us
  waiting for transfers between devices: 14.5 us -> 10.8 us
    all_to_all x1, starting transfers between devices: 13.7 us -> 10 us  [exchange(): lax.all_to_all(array, 'ctx', 0, 0, axis_index_groups=LANES, tiled=True)]
    ppermute x13, waiting for transfers between devices: 6.62 us -> 2.95 us  [body(): lax.ppermute(outgoing[kind], 'ctx', shift_pairs(SHIFTS[kind]))]
  transfers between devices with their start and end apart: 17 -> 17, of which waited for: 3 -> 2; matrix products, arithmetic and copies ran while one was open for 1% -> 1% of each run, Pallas kernels for 10% -> 11%
where the time goes in v1:
time: 326 us; the launch traced here: 322 us
  blocking collectives  204 us (63%)
  Pallas kernels  60.3 us (18%)
  starting transfers between devices  40.6 us (12%)
  waiting for transfers between devices  10.8 us (3%)
  local copies, waits for them, and re-layouts  5.16 us (2%)
    all_to_all x1, blocking collectives, exchange(): lax.all_to_all(array, 'ctx', 0, 0, axis_index_groups=LANES, tiled=True)  204 us
    pallas_call x4, Pallas kernels, attend(): pl.pallas_call(lambda *refs: attend_kernel(wave, kinds, *refs), in_specs=...  39.6 us
    ppermute x13, starting transfers between devices, body(): lax.ppermute(outgoing[kind], 'ctx', shift_pairs(SHIFTS[kind]))  19.3 us
    pallas_call x1, Pallas kernels, pack(): pl.pallas_call(pack_kernel, in_specs=[VMEM, SMEM, ANY, ANY, ANY, ANY], ou...  13.7 us
    all_to_all x1, starting transfers between devices, body(): chosen_all = lax.all_to_all(spread, 'ctx', 0, 0, tiled=True)  10.6 us
    all_to_all x1, starting transfers between devices, exchange(): lax.all_to_all(array, 'ctx', 0, 0, axis_index_groups=LANES, tiled=True)  10 us
    all_to_all x1, waiting for transfers between devices, body(): chosen_all = lax.all_to_all(spread, 'ctx', 0, 0, tiled=True)  7.87 us
    pallas_call x1, Pallas kernels, forward(): pl.pallas_call(forward_kernel, in_specs=[SMEM, SMEM, ANY], out_specs=[ANY...  7.09 us
  transfers between devices with their start and end apart: 17, of which 2 were waited for; matrix products, arithmetic and copies ran while one was open for 1% of the time, Pallas kernels for 11%

profile of v1, /device:TPU:7, one launch (start us, length us, event | category | flops | bytes accessed | tf_op | source)
XLA Modules:
  0.0 322.2 jit_solution(6005924753917393962)
XLA Ops:
  0.0 0.7 collective-permute-start
  0.7 0.0 collective-permute-start.1
  0.7 0.8 copy.30
  1.4 0.1 broadcast_in_dim.55
  1.5 0.7 broadcast_in_dim.56
  2.2 10.6 %all-to-all-start.2 = ((s32[128,1,48]{2,1,0:T(1,128)}), s32[128,1,48]{2,1,0:T(1,128)S(1)}, u32[]{:S(2)}, u32[]{:S(2)}) async-start(s32[128,1,48]{2,1,0:T(1,128)} %broadcast_in_dim.56), calls=%async_computation.2 | async-start | bytes 131072 | tf_op jit(solution)/shard_map/all_to_all | solution.py:592
  12.8 7.9 %all-to-all-done.2 = s32[128,1,48]{2,1,0:T(1,128)S(1)} async-done(((s32[128,1,48]{2,1,0:T(1,128)}), s32[128,1,48]{2,1,0:T(1,128)S(1)}, u32[]{:S(2)}, u32[]{:S(2)}) %all-to-all-start.2) | async-done | bytes 24608 | tf_op jit(solution)/shard_map/all_to_all | solution.py:592
  20.7 0.1 copy.31
  20.8 0.0 collective-permute-done
  20.8 0.0 copy-start.3
  20.8 0.0 collective-permute-done.1
  20.8 1.3 copy-done.3
  22.1 13.7 %pack.1 = (s32[248,128]{1,0:T(8,128)}, bf16[32,2,69,16,128]{4,3,2,1,0:T(8,128)(2,1)}, s32[148]{0:T(256)}) custom-call(s32[48,128]{1,0:T(8,128)S(1)} %bitcast.100, s32[1]{0:T(128)} %bitcast.13.me_ref, bf16[32,16,2048]{2,1,0:T(8,128)(2,1)} %bitcast.73, bf16[32,16,2048]{2,1,0:T(8,128)(2,1)} %bitcast.78, bf16[32,16,2048]{2,1,0:T(8,128)(2,1)} %bitcast.83, ...), custom_call_target="tpu_custom_call" | custom-call | tf_op jit(solution)/shard_map/pack/pallas_call | solution.py:294
  35.8 204.2 %all_to_all.28 = bf16[64,1104,128]{2,1,0:T(8,128)(2,1)} all-to-all(bf16[64,1104,128]{2,1,0:T(8,128)(2,1)} %bitcast.93), channel_id=1, replica_groups={{0,32,64,96,8,40,72,104,16,48,80,112,24,56,88,120,2,34,66,98,10,42,74,1..., dimensions={0} | all-to-all | bytes 36175872 | tf_op jit(solution)/shard_map/all_to_all | solution.py:556
  240.0 0.0 copy-start.1
  240.0 7.1 %forward.1 = (bf16[64,5,16,128]{3,2,1,0:T(8,128)(2,1)}, bf16[6,64,16,128]{3,2,1,0:T(8,128)(2,1)}, bf16[1,64,16,128]{3,2,1,0:T(8,128)(2,1)}, bf16[1,64,16,128]{3,...) custom-call(s32[248,128]{1,0:T(8,128)} %get-tuple-element.181.plan, ...), custom_call_target="tpu_custom_call" | custom-call | tf_op jit(solution)/shard_map/forward/pallas_call | solution.py:370
  247.1 2.4 collective-permute-start.2
  249.5 0.7 collective-permute-start.3
  250.2 1.1 collective-permute-start.4
  251.3 0.6 collective-permute-start.5
  251.9 1.1 collective-permute-start.6
  253.0 10.0 %all-to-all-start.4 = ((bf16[64,5,16,128]{3,2,1,0:T(8,128)(2,1)}), bf16[64,5,16,128]{3,2,1,0:T(8,128)(2,1)S(1)}, u32[]{:S(2)}, u32[]{:S(2)}) async-start(bf16[64,5,16,128]{3,2,1,0:T(8,128)(2,1)} %get-tuple-element.203), calls=%async_computation.4 | async-start | bytes 2621440 | tf_op jit(solution)/shard_map/all_to_all | solution.py:556
  263.0 0.0 copy-done.1
  263.0 16.9 %attend.4.refs_12_ = bf16[32,16,2048]{2,1,0:T(8,128)(2,1)} custom-call(s32[148]{0:T(256)} %get-tuple-element.182.refs_0_, bf16[32,16,2048]{2,1,0:T(8,128)(2,1)} %bitcast.88, bf16[32,16,2048]{2,1,0:T(8,128)(2,1)S(1)} %bitcast.74, bf16[32,16,2048]{2,1,0:T(8,128)(2,1)} %bitcast.79, bf16[32,16,2048]{2,1,0:T(8,128)(2,1)} %bitcast.84, ...), custom_call_target="tpu_custom_call" | custom-call | flops 19327352832 | bytes 3145728 | tf_op jit(solution)/shard_map/attend/pallas_call | solution.py:529
  279.9 1.2 slice.3
  281.7 0.0 collective-permute-done.3.refs_8_
  281.7 0.7 collective-permute-start.10
  282.5 0.0 collective-permute-done.4.refs_9_
  282.5 0.0 collective-permute-start.7
  282.5 0.0 collective-permute-done.5.refs_10_
  282.5 1.9 collective-permute-start.8
  284.4 0.0 collective-permute-done.6.refs_11_
  284.4 2.1 collective-permute-start.9
  286.5 0.0 collective-permute-done.2.refs_7_
  286.5 2.1 collective-permute-start.11
  288.6 10.1 %attend.5.refs_16_ = bf16[32,16,2048]{2,1,0:T(8,128)(2,1)} custom-call(s32[148]{0:T(256)} %get-tuple-element.182.refs_0_, bf16[32,16,2048]{2,1,0:T(8,128)(2,1)} %bitcast.89, bf16[32,16,2048]{2,1,0:T(8,128)(2,1)S(1)} %bitcast.75, bf16[32,16,2048]{2,1,0:T(8,128)(2,1)} %bitcast.80, bf16[32,16,2048]{2,1,0:T(8,128)(2,1)} %bitcast.85, ...), custom_call_target="tpu_custom_call", output_to_operand_aliasing={{}: (12, {})} | custom-call | flops 8589934592 | bytes 3145728 | tf_op jit(solution)/shard_map/attend/pallas_call | solution.py:529
  298.7 0.0 collective-permute-done.10.refs_15_
  298.7 0.0 copy-start.5
  298.7 1.2 collective-permute-start.12
  299.9 0.0 collective-permute-done.7.refs_12_
  299.9 0.0 copy-start.6
  299.9 5.4 %collective-permute-start.13 = (bf16[1,64,16,128]{3,2,1,0:T(8,128)(2,1)}, bf16[1,64,16,128]{3,2,1,0:T(8,128)(2,1)}, u32[]{:S(2)}, u32[]{:S(2)}) collective-permute-start(bf16[1,64,16,128]{3,2,1,0:T(8,128)(2,1)} %get-tuple-element.201), channel_id=1, source_target_pairs={{6,0},{7,1},{0,2},{1,3},{2,4},{3,5},{4,6},{5,7},{14,8},{15,9},{8,1... | collective-permute-start | bytes 786440 | tf_op jit(solution)/shard_map/ppermute | solution.py:607
  305.3 0.0 collective-permute-done.8.refs_13_
  305.3 0.0 collective-permute-start.14
  305.3 0.0 collective-permute-done.9.refs_14_
  305.3 0.0 copy-done.5
  305.3 0.0 copy-done.6
  305.3 8.1 %attend.6.refs_21_ = bf16[32,16,2048]{2,1,0:T(8,128)(2,1)} custom-call(s32[148]{0:T(256)} %get-tuple-element.182.refs_0_, bf16[32,16,2048]{2,1,0:T(8,128)(2,1)} %bitcast.90, bf16[32,16,2048]{2,1,0:T(8,128)(2,1)S(1)} %bitcast.76, bf16[32,16,2048]{2,1,0:T(8,128)(2,1)} %bitcast.81, bf16[32,16,2048]{2,1,0:T(8,128)(2,1)} %bitcast.86, ...), custom_call_target="tpu_custom_call", output_to_operand_aliasing={{}: (16, {})} | custom-call | flops 4294967296 | bytes 3145728 | tf_op jit(solution)/shard_map/attend/pallas_call | solution.py:529
  313.4 0.0 collective-permute-done.11.refs_16_
  313.4 0.0 collective-permute-done.12.refs_17_
  313.4 0.0 collective-permute-done.13.refs_18_
  313.5 2.9 collective-permute-done.14.refs_19_
  316.4 0.0 all-to-all-done.4
  316.4 0.0 copy-start.4
  316.4 1.1 copy-done.4
  317.4 4.5 %attend.7 = bf16[32,16,2048]{2,1,0:T(8,128)(2,1)} custom-call(s32[148]{0:T(256)} %get-tuple-element.182.refs_0_, bf16[32,16,2048]{2,1,0:T(8,128)(2,1)} %bitcast.91, bf16[32,16,2048]{2,1,0:T(8,128)(2,1)S(1)} %bitcast.77, bf16[32,16,2048]{2,1,0:T(8,128)(2,1)} %bitcast.82, bf16[32,16,2048]{2,1,0:T(8,128)(2,1)} %bitcast.87, ...), custom_call_target="tpu_custom_call", output_to_operand_aliasing={{}: (21, {})} | custom-call | flops 4294967296 | bytes 3145728 | tf_op jit(solution)/shard_map/attend/pallas_call | solution.py:529
  (1 shorter events, 0.0 us)
Async XLA Ops:
  0.0 20.8 %collective-permute-start = (bf16[512,2048]{1,0:T(8,128)(2,1)}, bf16[512,2048]{1,0:T(8,128)(2,1)S(1)}, u32[]{:S(2)}, u32[]{:S(2)}) collective-permute-start(bf16[512,2048]{1,0:T(8,128)(2,1)} %param.11), channel_id=1, source_target_pairs={{0,1},{1,0},{2,3},{3,2},{4,5},{5,4},{6,7},{7,6},{8,9},{9,8},{10,11... | collective-permute-start | bytes 6291464 | tf_op jit(solution)/shard_map/ppermute | solution.py:589
  0.7 20.1 %collective-permute-start.1 = (bf16[512,2048]{1,0:T(8,128)(2,1)}, bf16[512,2048]{1,0:T(8,128)(2,1)}, u32[]{:S(2)}, u32[]{:S(2)}) collective-permute-start(bf16[512,2048]{1,0:T(8,128)(2,1)} %param.12), channel_id=1, source_target_pairs={{0,1},{1,0},{2,3},{3,2},{4,5},{5,4},{6,7},{7,6},{8,9},{9,8},{10,11... | collective-permute-start | bytes 6291464 | tf_op jit(solution)/shard_map/ppermute | solution.py:590
  2.2 18.5 %all-to-all-start.2 = ((s32[128,1,48]{2,1,0:T(1,128)}), s32[128,1,48]{2,1,0:T(1,128)S(1)}, u32[]{:S(2)}, u32[]{:S(2)}) async-start(s32[128,1,48]{2,1,0:T(1,128)} %broadcast_in_dim.56), calls=%async_computation.2 | async-start | bytes 131072 | tf_op jit(solution)/shard_map/all_to_all | solution.py:592
  20.8 1.3 copy-start.3
  240.0 23.0 %copy-start.1 = (bf16[512,2048]{1,0:T(8,128)(2,1)S(1)}, bf16[512,2048]{1,0:T(8,128)(2,1)}, u32[]{:S(2)}) copy-start(bf16[512,2048]{1,0:T(8,128)(2,1)} %param.11) | copy-start | bytes 6291460
  247.1 39.4 %collective-permute-start.2 = (bf16[6,64,16,128]{3,2,1,0:T(8,128)(2,1)}, bf16[6,64,16,128]{3,2,1,0:T(8,128)(2,1)}, u32[]{:S(2)}, u32[]{:S(2)}) collective-permute-start(bf16[6,64,16,128]{3,2,1,0:T(8,128)(2,1)} %get-tuple-element.190), channel_id=1, source_target_pairs={{1,0},{0,1},{3,2},{2,3},{5,4},{4,5},{7,6},{6,7},{9,8},{8,9},{11,10... | collective-permute-start | bytes 4718600 | tf_op jit(solution)/shard_map/ppermute | solution.py:607
  249.5 32.2 %collective-permute-start.3 = (bf16[1,64,16,128]{3,2,1,0:T(8,128)(2,1)}, bf16[1,64,16,128]{3,2,1,0:T(8,128)(2,1)}, u32[]{:S(2)}, u32[]{:S(2)}) collective-permute-start(bf16[1,64,16,128]{3,2,1,0:T(8,128)(2,1)} %get-tuple-element.191), channel_id=1, source_target_pairs={{32,0},{33,1},{34,2},{35,3},{36,4},{37,5},{38,6},{39,7},{40,8},{41... | collective-permute-start | bytes 786440 | tf_op jit(solution)/shard_map/ppermute | solution.py:607
  250.2 32.3 %collective-permute-start.4 = (bf16[1,64,16,128]{3,2,1,0:T(8,128)(2,1)}, bf16[1,64,16,128]{3,2,1,0:T(8,128)(2,1)}, u32[]{:S(2)}, u32[]{:S(2)}) collective-permute-start(bf16[1,64,16,128]{3,2,1,0:T(8,128)(2,1)} %get-tuple-element.192), channel_id=1, source_target_pairs={{33,0},{32,1},{35,2},{34,3},{37,4},{36,5},{39,6},{38,7},{41,8},{40... | collective-permute-start | bytes 786440 | tf_op jit(solution)/shard_map/ppermute | solution.py:607
  251.3 31.2 %collective-permute-start.5 = (bf16[1,64,16,128]{3,2,1,0:T(8,128)(2,1)}, bf16[1,64,16,128]{3,2,1,0:T(8,128)(2,1)}, u32[]{:S(2)}, u32[]{:S(2)}) collective-permute-start(bf16[1,64,16,128]{3,2,1,0:T(8,128)(2,1)} %get-tuple-element.193), channel_id=1, source_target_pairs={{96,0},{97,1},{98,2},{99,3},{100,4},{101,5},{102,6},{103,7},{104,8... | collective-permute-start | bytes 786440 | tf_op jit(solution)/shard_map/ppermute | solution.py:607
  251.9 32.5 %collective-permute-start.6 = (bf16[1,64,16,128]{3,2,1,0:T(8,128)(2,1)}, bf16[1,64,16,128]{3,2,1,0:T(8,128)(2,1)}, u32[]{:S(2)}, u32[]{:S(2)}) collective-permute-start(bf16[1,64,16,128]{3,2,1,0:T(8,128)(2,1)} %get-tuple-element.194), channel_id=1, source_target_pairs={{97,0},{96,1},{99,2},{98,3},{101,4},{100,5},{103,6},{102,7},{105,8... | collective-permute-start | bytes 786440 | tf_op jit(solution)/shard_map/ppermute | solution.py:607
  253.0 63.4 %all-to-all-start.4 = ((bf16[64,5,16,128]{3,2,1,0:T(8,128)(2,1)}), bf16[64,5,16,128]{3,2,1,0:T(8,128)(2,1)S(1)}, u32[]{:S(2)}, u32[]{:S(2)}) async-start(bf16[64,5,16,128]{3,2,1,0:T(8,128)(2,1)} %get-tuple-element.203), calls=%async_computation.4 | async-start | bytes 2621440 | tf_op jit(solution)/shard_map/all_to_all | solution.py:556
  281.7 17.0 %collective-permute-start.10 = (bf16[1,64,16,128]{3,2,1,0:T(8,128)(2,1)}, bf16[1,64,16,128]{3,2,1,0:T(8,128)(2,1)S(1)}, u32[]{:S(2)}, u32[]{:S(2)}) collective-permute-start(bf16[1,64,16,128]{3,2,1,0:T(8,128)(2,1)} %get-tuple-element.198), channel_id=1, source_target_pairs={{25,0},{24,1},{27,2},{26,3},{29,4},{28,5},{31,6},{30,7},{1,8},{0,9... | collective-permute-start | bytes 786440 | tf_op jit(solution)/shard_map/ppermute | solution.py:607
  282.5 17.4 %collective-permute-start.7 = (bf16[1,64,16,128]{3,2,1,0:T(8,128)(2,1)}, bf16[1,64,16,128]{3,2,1,0:T(8,128)(2,1)S(1)}, u32[]{:S(2)}, u32[]{:S(2)}) collective-permute-start(bf16[1,64,16,128]{3,2,1,0:T(8,128)(2,1)} %get-tuple-element.195), channel_id=1, source_target_pairs={{8,0},{9,1},{10,2},{11,3},{12,4},{13,5},{14,6},{15,7},{16,8},{17,9... | collective-permute-start | bytes 786440 | tf_op jit(solution)/shard_map/ppermute | solution.py:607
  282.5 22.8 %collective-permute-start.8 = (bf16[1,64,16,128]{3,2,1,0:T(8,128)(2,1)}, bf16[1,64,16,128]{3,2,1,0:T(8,128)(2,1)}, u32[]{:S(2)}, u32[]{:S(2)}) collective-permute-start(bf16[1,64,16,128]{3,2,1,0:T(8,128)(2,1)} %get-tuple-element.196), channel_id=1, source_target_pairs={{9,0},{8,1},{11,2},{10,3},{13,4},{12,5},{15,6},{14,7},{17,8},{16,9... | collective-permute-start | bytes 786440 | tf_op jit(solution)/shard_map/ppermute | solution.py:607
  284.4 20.9 %collective-permute-start.9 = (bf16[1,64,16,128]{3,2,1,0:T(8,128)(2,1)}, bf16[1,64,16,128]{3,2,1,0:T(8,128)(2,1)}, u32[]{:S(2)}, u32[]{:S(2)}) collective-permute-start(bf16[1,64,16,128]{3,2,1,0:T(8,128)(2,1)} %get-tuple-element.197), channel_id=1, source_target_pairs={{24,0},{25,1},{26,2},{27,3},{28,4},{29,5},{30,6},{31,7},{0,8},{1,9... | collective-permute-start | bytes 786440 | tf_op jit(solution)/shard_map/ppermute | solution.py:607
  286.5 26.9 %collective-permute-start.11 = (bf16[1,64,16,128]{3,2,1,0:T(8,128)(2,1)}, bf16[1,64,16,128]{3,2,1,0:T(8,128)(2,1)}, u32[]{:S(2)}, u32[]{:S(2)}) collective-permute-start(bf16[1,64,16,128]{3,2,1,0:T(8,128)(2,1)} %get-tuple-element.199), channel_id=1, source_target_pairs={{2,0},{3,1},{4,2},{5,3},{6,4},{7,5},{0,6},{1,7},{10,8},{11,9},{12,... | collective-permute-start | bytes 786440 | tf_op jit(solution)/shard_map/ppermute | solution.py:607
  298.7 6.6 %copy-start.5 = (bf16[1,64,16,128]{3,2,1,0:T(8,128)(2,1)}, bf16[1,64,16,128]{3,2,1,0:T(8,128)(2,1)S(1)}, u32[]{:S(2)}) copy-start(bf16[1,64,16,128]{3,2,1,0:T(8,128)(2,1)S(1)} %collective-permute-done.10.refs_15_) | copy-start | bytes 786436
  298.7 14.7 %collective-permute-start.12 = (bf16[1,64,16,128]{3,2,1,0:T(8,128)(2,1)}, bf16[1,64,16,128]{3,2,1,0:T(8,128)(2,1)}, u32[]{:S(2)}, u32[]{:S(2)}) collective-permute-start(bf16[1,64,16,128]{3,2,1,0:T(8,128)(2,1)} %get-tuple-element.200), channel_id=1, source_target_pairs={{3,0},{2,1},{5,2},{4,3},{7,4},{6,5},{1,6},{0,7},{11,8},{10,9},{13,... | collective-permute-start | bytes 786440 | tf_op jit(solution)/shard_map/ppermute | solution.py:607
  299.9 5.4 %copy-start.6 = (bf16[1,64,16,128]{3,2,1,0:T(8,128)(2,1)}, bf16[1,64,16,128]{3,2,1,0:T(8,128)(2,1)S(1)}, u32[]{:S(2)}) copy-start(bf16[1,64,16,128]{3,2,1,0:T(8,128)(2,1)S(1)} %collective-permute-done.7.refs_12_) | copy-start | bytes 786436
  299.9 13.6 %collective-permute-start.13 = (bf16[1,64,16,128]{3,2,1,0:T(8,128)(2,1)}, bf16[1,64,16,128]{3,2,1,0:T(8,128)(2,1)}, u32[]{:S(2)}, u32[]{:S(2)}) collective-permute-start(bf16[1,64,16,128]{3,2,1,0:T(8,128)(2,1)} %get-tuple-element.201), channel_id=1, source_target_pairs={{6,0},{7,1},{0,2},{1,3},{2,4},{3,5},{4,6},{5,7},{14,8},{15,9},{8,1... | collective-permute-start | bytes 786440 | tf_op jit(solution)/shard_map/ppermute | solution.py:607
  305.3 11.1 %collective-permute-start.14 = (bf16[1,64,16,128]{3,2,1,0:T(8,128)(2,1)}, bf16[1,64,16,128]{3,2,1,0:T(8,128)(2,1)}, u32[]{:S(2)}, u32[]{:S(2)}) collective-permute-start(bf16[1,64,16,128]{3,2,1,0:T(8,128)(2,1)} %get-tuple-element.202), channel_id=1, source_target_pairs={{7,0},{6,1},{1,2},{0,3},{3,4},{2,5},{5,6},{4,7},{15,8},{14,9},{9,1... | collective-permute-start | bytes 786440 | tf_op jit(solution)/shard_map/ppermute | solution.py:607
  316.4 1.1 copy-start.4

commit v2 on v1

--- a/solution.py
+++ b/solution.py
@@ -17,7 +17,7 @@
 ONE = [(1, 0, 0), (3, 0, 0), (0, 1, 0), (0, 3, 0), (0, 0, 1), (0, 0, 3)]
 PARTNER = 6
 SHIFTS = [(0, 0, 0, 1)] * PARTNER
-SHIFTS += [(*s, c) for s in ONE for c in (0, 1)]
+SHIFTS += [(*s, c) for c in (0, 1) for s in ONE]
 KINDS = len(SHIFTS)
 SPARE = 5
 PIECE = 16

time: 326 us -> 328 us (level); the launches traced: 322 us -> 328 us
  starting transfers between devices: 40.6 us -> 44.6 us
    ppermute x13, starting transfers between devices: 19.3 us -> 26.4 us  [body(): lax.ppermute(outgoing[kind], 'ctx', shift_pairs(SHIFTS[kind]))]
  transfers between devices with their start and end apart: 17 -> 17, of which waited for: 2 -> 2; matrix products, arithmetic and copies ran while one was open for 1% -> 1% of each run, Pallas kernels for 11% -> 9%
where the time goes in v2:
time: 328 us
  blocking collectives  205 us (62%)
  Pallas kernels  60.7 us (19%)
  starting transfers between devices  44.6 us (14%)
  waiting for transfers between devices  11.6 us (4%)
  local copies, waits for them, and re-layouts  5.16 us (2%)
    all_to_all x1, blocking collectives, exchange(): lax.all_to_all(array, 'ctx', 0, 0, axis_index_groups=LANES, tiled=True)  205 us
    pallas_call x4, Pallas kernels, attend(): pl.pallas_call(lambda *refs: attend_kernel(wave, kinds, *refs), in_specs=...  39.6 us
    ppermute x13, starting transfers between devices, body(): lax.ppermute(outgoing[kind], 'ctx', shift_pairs(SHIFTS[kind]))  26.4 us
    pallas_call x1, Pallas kernels, pack(): pl.pallas_call(pack_kernel, in_specs=[VMEM, SMEM, ANY, ANY, ANY, ANY], ou...  13.6 us
    all_to_all x1, starting transfers between devices, body(): chosen_all = lax.all_to_all(spread, 'ctx', 0, 0, tiled=True)  10.6 us
    all_to_all x1, waiting for transfers between devices, body(): chosen_all = lax.all_to_all(spread, 'ctx', 0, 0, tiled=True)  7.87 us
    pallas_call x1, Pallas kernels, forward(): pl.pallas_call(forward_kernel, in_specs=[SMEM, SMEM, ANY], out_specs=[ANY...  7.44 us
    all_to_all x1, starting transfers between devices, exchange(): lax.all_to_all(array, 'ctx', 0, 0, axis_index_groups=LANES, tiled=True)  6.9 us
  transfers between devices with their start and end apart: 17, of which 2 were waited for; matrix products, arithmetic and copies ran while one was open for 1% of the time, Pallas kernels for 9%

profile of v2, /device:TPU:7, one launch (start us, length us, event | category | flops | bytes accessed | tf_op | source)
XLA Modules:
  0.0 327.9 jit_solution(13428153671826683433)
XLA Ops:
  0.0 0.7 collective-permute-start
  0.7 0.0 collective-permute-start.1
  0.7 0.8 copy.30
  1.4 0.1 broadcast_in_dim.55
  1.5 0.7 broadcast_in_dim.56
  2.2 10.6 %all-to-all-start.2 = ((s32[128,1,48]{2,1,0:T(1,128)}), s32[128,1,48]{2,1,0:T(1,128)S(1)}, u32[]{:S(2)}, u32[]{:S(2)}) async-start(s32[128,1,48]{2,1,0:T(1,128)} %broadcast_in_dim.56), calls=%async_computation.2 | async-start | bytes 131072 | tf_op jit(solution)/shard_map/all_to_all | solution.py:592
  12.8 7.9 %all-to-all-done.2 = s32[128,1,48]{2,1,0:T(1,128)S(1)} async-done(((s32[128,1,48]{2,1,0:T(1,128)}), s32[128,1,48]{2,1,0:T(1,128)S(1)}, u32[]{:S(2)}, u32[]{:S(2)}) %all-to-all-start.2) | async-done | bytes 24608 | tf_op jit(solution)/shard_map/all_to_all | solution.py:592
  20.7 0.1 copy.31
  20.8 0.0 collective-permute-done
  20.8 0.0 copy-start.3
  20.8 0.0 collective-permute-done.1
  20.8 1.3 copy-done.3
  22.1 13.6 %pack.1 = (s32[248,128]{1,0:T(8,128)}, bf16[32,2,69,16,128]{4,3,2,1,0:T(8,128)(2,1)}, s32[148]{0:T(256)}) custom-call(s32[48,128]{1,0:T(8,128)S(1)} %bitcast.100, s32[1]{0:T(128)} %bitcast.13.me_ref, bf16[32,16,2048]{2,1,0:T(8,128)(2,1)} %bitcast.73, bf16[32,16,2048]{2,1,0:T(8,128)(2,1)} %bitcast.78, bf16[32,16,2048]{2,1,0:T(8,128)(2,1)} %bitcast.83, ...), custom_call_target="tpu_custom_call" | custom-call | tf_op jit(solution)/shard_map/pack/pallas_call | solution.py:294
  35.7 204.9 %all_to_all.28 = bf16[64,1104,128]{2,1,0:T(8,128)(2,1)} all-to-all(bf16[64,1104,128]{2,1,0:T(8,128)(2,1)} %bitcast.93), channel_id=1, replica_groups={{0,32,64,96,8,40,72,104,16,48,80,112,24,56,88,120,2,34,66,98,10,42,74,1..., dimensions={0} | all-to-all | bytes 36175872 | tf_op jit(solution)/shard_map/all_to_all | solution.py:556
  240.6 0.0 copy-start.1
  240.6 7.4 %forward.1 = (bf16[64,5,16,128]{3,2,1,0:T(8,128)(2,1)}, bf16[6,64,16,128]{3,2,1,0:T(8,128)(2,1)}, bf16[1,64,16,128]{3,2,1,0:T(8,128)(2,1)}, bf16[1,64,16,128]{3,...) custom-call(s32[248,128]{1,0:T(8,128)} %get-tuple-element.181.plan, ...), custom_call_target="tpu_custom_call" | custom-call | tf_op jit(solution)/shard_map/forward/pallas_call | solution.py:370
  248.0 1.4 collective-permute-start.2
  249.4 1.9 collective-permute-start.3
  251.4 0.0 collective-permute-start.4
  251.4 6.2 %collective-permute-start.5 = (bf16[1,64,16,128]{3,2,1,0:T(8,128)(2,1)}, bf16[1,64,16,128]{3,2,1,0:T(8,128)(2,1)}, u32[]{:S(2)}, u32[]{:S(2)}) collective-permute-start(bf16[1,64,16,128]{3,2,1,0:T(8,128)(2,1)} %get-tuple-element.193), channel_id=1, source_target_pairs={{8,0},{9,1},{10,2},{11,3},{12,4},{13,5},{14,6},{15,7},{16,8},{17,9... | collective-permute-start | bytes 786440 | tf_op jit(solution)/shard_map/ppermute | solution.py:607
  257.6 0.0 collective-permute-start.6
  257.6 6.9 %all-to-all-start.4 = ((bf16[64,5,16,128]{3,2,1,0:T(8,128)(2,1)}), bf16[64,5,16,128]{3,2,1,0:T(8,128)(2,1)S(1)}, u32[]{:S(2)}, u32[]{:S(2)}) async-start(bf16[64,5,16,128]{3,2,1,0:T(8,128)(2,1)} %get-tuple-element.203), calls=%async_computation.4 | async-start | bytes 2621440 | tf_op jit(solution)/shard_map/all_to_all | solution.py:556
  264.5 0.0 copy-done.1
  264.5 15.1 %attend.4.refs_12_ = bf16[32,16,2048]{2,1,0:T(8,128)(2,1)} custom-call(s32[148]{0:T(256)} %get-tuple-element.182.refs_0_, bf16[32,16,2048]{2,1,0:T(8,128)(2,1)} %bitcast.88, bf16[32,16,2048]{2,1,0:T(8,128)(2,1)S(1)} %bitcast.74, bf16[32,16,2048]{2,1,0:T(8,128)(2,1)} %bitcast.79, bf16[32,16,2048]{2,1,0:T(8,128)(2,1)} %bitcast.84, ...), custom_call_target="tpu_custom_call" | custom-call | flops 19327352832 | bytes 3145728 | tf_op jit(solution)/shard_map/attend/pallas_call | solution.py:529
  279.6 1.2 slice.3
  281.5 0.0 collective-permute-done.3.refs_8_
  281.5 4.8 %collective-permute-start.10 = (bf16[1,64,16,128]{3,2,1,0:T(8,128)(2,1)}, bf16[1,64,16,128]{3,2,1,0:T(8,128)(2,1)S(1)}, u32[]{:S(2)}, u32[]{:S(2)}) collective-permute-start(bf16[1,64,16,128]{3,2,1,0:T(8,128)(2,1)} %get-tuple-element.198), channel_id=1, source_target_pairs={{97,0},{96,1},{99,2},{98,3},{101,4},{100,5},{103,6},{102,7},{105,8... | collective-permute-start | bytes 786440 | tf_op jit(solution)/shard_map/ppermute | solution.py:607
  286.3 0.0 collective-permute-done.4.refs_9_
  286.3 0.9 collective-permute-start.7
  287.2 0.0 collective-permute-done.5.refs_10_
  287.2 0.6 collective-permute-start.8
  287.8 0.0 collective-permute-done.6.refs_11_
  287.8 2.9 collective-permute-start.9
  290.7 0.0 collective-permute-done.2.refs_7_
  290.7 0.7 collective-permute-start.11
  291.4 8.3 %attend.5.refs_16_ = bf16[32,16,2048]{2,1,0:T(8,128)(2,1)} custom-call(s32[148]{0:T(256)} %get-tuple-element.182.refs_0_, bf16[32,16,2048]{2,1,0:T(8,128)(2,1)} %bitcast.89, bf16[32,16,2048]{2,1,0:T(8,128)(2,1)S(1)} %bitcast.75, bf16[32,16,2048]{2,1,0:T(8,128)(2,1)} %bitcast.80, bf16[32,16,2048]{2,1,0:T(8,128)(2,1)} %bitcast.85, ...), custom_call_target="tpu_custom_call", output_to_operand_aliasing={{}: (12, {})} | custom-call | flops 8589934592 | bytes 3145728 | tf_op jit(solution)/shard_map/attend/pallas_call | solution.py:529
  299.7 0.0 collective-permute-done.10.refs_15_
  299.7 0.0 copy-start.5
  299.7 4.1 %collective-permute-start.12 = (bf16[1,64,16,128]{3,2,1,0:T(8,128)(2,1)}, bf16[1,64,16,128]{3,2,1,0:T(8,128)(2,1)}, u32[]{:S(2)}, u32[]{:S(2)}) collective-permute-start(bf16[1,64,16,128]{3,2,1,0:T(8,128)(2,1)} %get-tuple-element.200), channel_id=1, source_target_pairs={{25,0},{24,1},{27,2},{26,3},{29,4},{28,5},{31,6},{30,7},{1,8},{0,9... | collective-permute-start | bytes 786440 | tf_op jit(solution)/shard_map/ppermute | solution.py:607
  303.8 0.0 collective-permute-done.7.refs_12_
  303.8 0.0 copy-start.6
  303.8 2.8 collective-permute-start.13
  306.6 0.0 collective-permute-done.8.refs_13_
  306.6 0.0 collective-permute-start.14
  306.6 0.0 collective-permute-done.9.refs_14_
  306.6 0.0 copy-done.5
  306.6 0.0 copy-done.6
  306.6 6.3 %attend.6.refs_21_ = bf16[32,16,2048]{2,1,0:T(8,128)(2,1)} custom-call(s32[148]{0:T(256)} %get-tuple-element.182.refs_0_, bf16[32,16,2048]{2,1,0:T(8,128)(2,1)} %bitcast.90, bf16[32,16,2048]{2,1,0:T(8,128)(2,1)S(1)} %bitcast.76, bf16[32,16,2048]{2,1,0:T(8,128)(2,1)} %bitcast.81, bf16[32,16,2048]{2,1,0:T(8,128)(2,1)} %bitcast.86, ...), custom_call_target="tpu_custom_call", output_to_operand_aliasing={{}: (16, {})} | custom-call | flops 4294967296 | bytes 3145728 | tf_op jit(solution)/shard_map/attend/pallas_call | solution.py:529
  312.9 0.0 collective-permute-done.11.refs_16_
  312.9 0.0 collective-permute-done.12.refs_17_
  312.9 0.0 collective-permute-done.13.refs_18_
  312.9 3.7 %collective-permute-done.14.refs_19_ = bf16[1,64,16,128]{3,2,1,0:T(8,128)(2,1)} collective-permute-done((bf16[1,64,16,128]{3,2,1,0:T(8,128)(2,1)}, bf16[1,64,16,128]{3,2,1,0:T(8,128)(2,1)}, u32[]{:S(2)}, u32[]{:S(2)}) %collective-permute-start.14) | collective-permute-done | bytes 262176 | tf_op jit(solution)/shard_map/ppermute | solution.py:607
  316.7 0.0 all-to-all-done.4
  316.7 0.0 copy-start.4
  316.7 1.1 copy-done.4
  317.7 10.0 %attend.7 = bf16[32,16,2048]{2,1,0:T(8,128)(2,1)} custom-call(s32[148]{0:T(256)} %get-tuple-element.182.refs_0_, bf16[32,16,2048]{2,1,0:T(8,128)(2,1)} %bitcast.91, bf16[32,16,2048]{2,1,0:T(8,128)(2,1)S(1)} %bitcast.77, bf16[32,16,2048]{2,1,0:T(8,128)(2,1)} %bitcast.82, bf16[32,16,2048]{2,1,0:T(8,128)(2,1)} %bitcast.87, ...), custom_call_target="tpu_custom_call", output_to_operand_aliasing={{}: (21, {})} | custom-call | flops 4294967296 | bytes 3145728 | tf_op jit(solution)/shard_map/attend/pallas_call | solution.py:529
  (1 shorter events, 0.0 us)
Async XLA Ops:
  0.0 20.8 %collective-permute-start = (bf16[512,2048]{1,0:T(8,128)(2,1)}, bf16[512,2048]{1,0:T(8,128)(2,1)S(1)}, u32[]{:S(2)}, u32[]{:S(2)}) collective-permute-start(bf16[512,2048]{1,0:T(8,128)(2,1)} %param.11), channel_id=1, source_target_pairs={{0,1},{1,0},{2,3},{3,2},{4,5},{5,4},{6,7},{7,6},{8,9},{9,8},{10,11... | collective-permute-start | bytes 6291464 | tf_op jit(solution)/shard_map/ppermute | solution.py:589
  0.7 20.1 %collective-permute-start.1 = (bf16[512,2048]{1,0:T(8,128)(2,1)}, bf16[512,2048]{1,0:T(8,128)(2,1)}, u32[]{:S(2)}, u32[]{:S(2)}) collective-permute-start(bf16[512,2048]{1,0:T(8,128)(2,1)} %param.12), channel_id=1, source_target_pairs={{0,1},{1,0},{2,3},{3,2},{4,5},{5,4},{6,7},{7,6},{8,9},{9,8},{10,11... | collective-permute-start | bytes 6291464 | tf_op jit(solution)/shard_map/ppermute | solution.py:590
  2.2 18.5 %all-to-all-start.2 = ((s32[128,1,48]{2,1,0:T(1,128)}), s32[128,1,48]{2,1,0:T(1,128)S(1)}, u32[]{:S(2)}, u32[]{:S(2)}) async-start(s32[128,1,48]{2,1,0:T(1,128)} %broadcast_in_dim.56), calls=%async_computation.2 | async-start | bytes 131072 | tf_op jit(solution)/shard_map/all_to_all | solution.py:592
  20.8 1.3 copy-start.3
  240.6 23.9 %copy-start.1 = (bf16[512,2048]{1,0:T(8,128)(2,1)S(1)}, bf16[512,2048]{1,0:T(8,128)(2,1)}, u32[]{:S(2)}) copy-start(bf16[512,2048]{1,0:T(8,128)(2,1)} %param.11) | copy-start | bytes 6291460
  248.0 42.6 %collective-permute-start.2 = (bf16[6,64,16,128]{3,2,1,0:T(8,128)(2,1)}, bf16[6,64,16,128]{3,2,1,0:T(8,128)(2,1)}, u32[]{:S(2)}, u32[]{:S(2)}) collective-permute-start(bf16[6,64,16,128]{3,2,1,0:T(8,128)(2,1)} %get-tuple-element.190), channel_id=1, source_target_pairs={{1,0},{0,1},{3,2},{2,3},{5,4},{4,5},{7,6},{6,7},{9,8},{8,9},{11,10... | collective-permute-start | bytes 4718600 | tf_op jit(solution)/shard_map/ppermute | solution.py:607
  249.4 32.0 %collective-permute-start.3 = (bf16[1,64,16,128]{3,2,1,0:T(8,128)(2,1)}, bf16[1,64,16,128]{3,2,1,0:T(8,128)(2,1)}, u32[]{:S(2)}, u32[]{:S(2)}) collective-permute-start(bf16[1,64,16,128]{3,2,1,0:T(8,128)(2,1)} %get-tuple-element.191), channel_id=1, source_target_pairs={{32,0},{33,1},{34,2},{35,3},{36,4},{37,5},{38,6},{39,7},{40,8},{41... | collective-permute-start | bytes 786440 | tf_op jit(solution)/shard_map/ppermute | solution.py:607
  251.4 34.9 %collective-permute-start.4 = (bf16[1,64,16,128]{3,2,1,0:T(8,128)(2,1)}, bf16[1,64,16,128]{3,2,1,0:T(8,128)(2,1)}, u32[]{:S(2)}, u32[]{:S(2)}) collective-permute-start(bf16[1,64,16,128]{3,2,1,0:T(8,128)(2,1)} %get-tuple-element.192), channel_id=1, source_target_pairs={{96,0},{97,1},{98,2},{99,3},{100,4},{101,5},{102,6},{103,7},{104,8... | collective-permute-start | bytes 786440 | tf_op jit(solution)/shard_map/ppermute | solution.py:607
  251.4 35.9 %collective-permute-start.5 = (bf16[1,64,16,128]{3,2,1,0:T(8,128)(2,1)}, bf16[1,64,16,128]{3,2,1,0:T(8,128)(2,1)}, u32[]{:S(2)}, u32[]{:S(2)}) collective-permute-start(bf16[1,64,16,128]{3,2,1,0:T(8,128)(2,1)} %get-tuple-element.193), channel_id=1, source_target_pairs={{8,0},{9,1},{10,2},{11,3},{12,4},{13,5},{14,6},{15,7},{16,8},{17,9... | collective-permute-start | bytes 786440 | tf_op jit(solution)/shard_map/ppermute | solution.py:607
  257.6 30.2 %collective-permute-start.6 = (bf16[1,64,16,128]{3,2,1,0:T(8,128)(2,1)}, bf16[1,64,16,128]{3,2,1,0:T(8,128)(2,1)}, u32[]{:S(2)}, u32[]{:S(2)}) collective-permute-start(bf16[1,64,16,128]{3,2,1,0:T(8,128)(2,1)} %get-tuple-element.194), channel_id=1, source_target_pairs={{24,0},{25,1},{26,2},{27,3},{28,4},{29,5},{30,6},{31,7},{0,8},{1,9... | collective-permute-start | bytes 786440 | tf_op jit(solution)/shard_map/ppermute | solution.py:607
  257.6 59.0 %all-to-all-start.4 = ((bf16[64,5,16,128]{3,2,1,0:T(8,128)(2,1)}), bf16[64,5,16,128]{3,2,1,0:T(8,128)(2,1)S(1)}, u32[]{:S(2)}, u32[]{:S(2)}) async-start(bf16[64,5,16,128]{3,2,1,0:T(8,128)(2,1)} %get-tuple-element.203), calls=%async_computation.4 | async-start | bytes 2621440 | tf_op jit(solution)/shard_map/all_to_all | solution.py:556
  281.5 18.2 %collective-permute-start.10 = (bf16[1,64,16,128]{3,2,1,0:T(8,128)(2,1)}, bf16[1,64,16,128]{3,2,1,0:T(8,128)(2,1)S(1)}, u32[]{:S(2)}, u32[]{:S(2)}) collective-permute-start(bf16[1,64,16,128]{3,2,1,0:T(8,128)(2,1)} %get-tuple-element.198), channel_id=1, source_target_pairs={{97,0},{96,1},{99,2},{98,3},{101,4},{100,5},{103,6},{102,7},{105,8... | collective-permute-start | bytes 786440 | tf_op jit(solution)/shard_map/ppermute | solution.py:607
  286.3 17.5 %collective-permute-start.7 = (bf16[1,64,16,128]{3,2,1,0:T(8,128)(2,1)}, bf16[1,64,16,128]{3,2,1,0:T(8,128)(2,1)S(1)}, u32[]{:S(2)}, u32[]{:S(2)}) collective-permute-start(bf16[1,64,16,128]{3,2,1,0:T(8,128)(2,1)} %get-tuple-element.195), channel_id=1, source_target_pairs={{2,0},{3,1},{4,2},{5,3},{6,4},{7,5},{0,6},{1,7},{10,8},{11,9},{12,... | collective-permute-start | bytes 786440 | tf_op jit(solution)/shard_map/ppermute | solution.py:607
  287.2 19.4 %collective-permute-start.8 = (bf16[1,64,16,128]{3,2,1,0:T(8,128)(2,1)}, bf16[1,64,16,128]{3,2,1,0:T(8,128)(2,1)}, u32[]{:S(2)}, u32[]{:S(2)}) collective-permute-start(bf16[1,64,16,128]{3,2,1,0:T(8,128)(2,1)} %get-tuple-element.196), channel_id=1, source_target_pairs={{6,0},{7,1},{0,2},{1,3},{2,4},{3,5},{4,6},{5,7},{14,8},{15,9},{8,1... | collective-permute-start | bytes 786440 | tf_op jit(solution)/shard_map/ppermute | solution.py:607
  287.8 18.8 %collective-permute-start.9 = (bf16[1,64,16,128]{3,2,1,0:T(8,128)(2,1)}, bf16[1,64,16,128]{3,2,1,0:T(8,128)(2,1)}, u32[]{:S(2)}, u32[]{:S(2)}) collective-permute-start(bf16[1,64,16,128]{3,2,1,0:T(8,128)(2,1)} %get-tuple-element.197), channel_id=1, source_target_pairs={{33,0},{32,1},{35,2},{34,3},{37,4},{36,5},{39,6},{38,7},{41,8},{40... | collective-permute-start | bytes 786440 | tf_op jit(solution)/shard_map/ppermute | solution.py:607
  290.7 22.2 %collective-permute-start.11 = (bf16[1,64,16,128]{3,2,1,0:T(8,128)(2,1)}, bf16[1,64,16,128]{3,2,1,0:T(8,128)(2,1)}, u32[]{:S(2)}, u32[]{:S(2)}) collective-permute-start(bf16[1,64,16,128]{3,2,1,0:T(8,128)(2,1)} %get-tuple-element.199), channel_id=1, source_target_pairs={{9,0},{8,1},{11,2},{10,3},{13,4},{12,5},{15,6},{14,7},{17,8},{16,9... | collective-permute-start | bytes 786440 | tf_op jit(solution)/shard_map/ppermute | solution.py:607
  299.7 6.9 %copy-start.5 = (bf16[1,64,16,128]{3,2,1,0:T(8,128)(2,1)}, bf16[1,64,16,128]{3,2,1,0:T(8,128)(2,1)S(1)}, u32[]{:S(2)}) copy-start(bf16[1,64,16,128]{3,2,1,0:T(8,128)(2,1)S(1)} %collective-permute-done.10.refs_15_) | copy-start | bytes 786436
  299.7 13.2 %collective-permute-start.12 = (bf16[1,64,16,128]{3,2,1,0:T(8,128)(2,1)}, bf16[1,64,16,128]{3,2,1,0:T(8,128)(2,1)}, u32[]{:S(2)}, u32[]{:S(2)}) collective-permute-start(bf16[1,64,16,128]{3,2,1,0:T(8,128)(2,1)} %get-tuple-element.200), channel_id=1, source_target_pairs={{25,0},{24,1},{27,2},{26,3},{29,4},{28,5},{31,6},{30,7},{1,8},{0,9... | collective-permute-start | bytes 786440 | tf_op jit(solution)/shard_map/ppermute | solution.py:607
  303.8 2.8 copy-start.6
  303.8 9.1 %collective-permute-start.13 = (bf16[1,64,16,128]{3,2,1,0:T(8,128)(2,1)}, bf16[1,64,16,128]{3,2,1,0:T(8,128)(2,1)}, u32[]{:S(2)}, u32[]{:S(2)}) collective-permute-start(bf16[1,64,16,128]{3,2,1,0:T(8,128)(2,1)} %get-tuple-element.201), channel_id=1, source_target_pairs={{3,0},{2,1},{5,2},{4,3},{7,4},{6,5},{1,6},{0,7},{11,8},{10,9},{13,... | collective-permute-start | bytes 786440 | tf_op jit(solution)/shard_map/ppermute | solution.py:607
  306.6 10.0 %collective-permute-start.14 = (bf16[1,64,16,128]{3,2,1,0:T(8,128)(2,1)}, bf16[1,64,16,128]{3,2,1,0:T(8,128)(2,1)}, u32[]{:S(2)}, u32[]{:S(2)}) collective-permute-start(bf16[1,64,16,128]{3,2,1,0:T(8,128)(2,1)} %get-tuple-element.202), channel_id=1, source_target_pairs={{7,0},{6,1},{1,2},{0,3},{3,4},{2,5},{5,6},{4,7},{15,8},{14,9},{9,1... | collective-permute-start | bytes 786440 | tf_op jit(solution)/shard_map/ppermute | solution.py:607
  316.7 1.1 copy-start.4

commit v3 on v2

--- a/solution.py
+++ b/solution.py
@@ -201,7 +201,7 @@
 
 
 def pack_kernel(chosen, me_ref, keys_in, values_in, other_keys_in, other_values_in, *rest):
-    plan_out, send, table, plan, keys, values, other_keys, other_values, sem, sems = rest
+    plan_out, send, table, left, plan, keys, values, other_keys, other_values, sem, sems = rest
     loads = []
     pairs = zip(
         (keys_in, values_in, other_keys_in, other_values_in),
@@ -265,6 +265,7 @@
     started = lax.fori_loop(0, CHIPS, one_slot, 0)
     started = lax.fori_loop(0, SPARE, one_spare, started)
     make_table(plan, me, table)
+    left[0] = plan[ROW_LEFT, 0]
 
     def wait_one(index, carry):
         pltpu.make_async_copy(
@@ -294,11 +295,12 @@
     return pl.pallas_call(
         pack_kernel,
         in_specs=[VMEM, SMEM, ANY, ANY, ANY, ANY],
-        out_specs=[VMEM, ANY, SMEM],
+        out_specs=[VMEM, ANY, SMEM, SMEM],
         out_shape=[
             jax.ShapeDtypeStruct((ROWS, DEVICES), jnp.int32),
             jax.ShapeDtypeStruct((HALF, 2, SLOT_PIECES, PIECE, HEAD), jnp.bfloat16),
             jax.ShapeDtypeStruct((TABLE,), jnp.int32),
+            jax.ShapeDtypeStruct((1,), jnp.int32),
         ],
         scratch_shapes=[pltpu.SMEM((ROWS, DEVICES), jnp.int32)]
         + [whole] * 4
@@ -590,11 +592,11 @@
     other_values = lax.ppermute(values, "ctx", SWAP)
     spread = jnp.broadcast_to(chosen.reshape(1, 3 * HEADS), (DEVICES, 3 * HEADS))
     chosen_all = lax.all_to_all(spread, "ctx", 0, 0, tiled=True)
-    plan, send, table = pack(chosen_all.T, me_ref, keys, values, other_keys, other_values)
+    plan, send, table, left = pack(chosen_all.T, me_ref, keys, values, other_keys, other_values)
     sent = exchange(send.reshape(CHIPS, SLOT_ROWS, HEAD))
-    held = (sent, plan, table, queries, keys, values, other_keys, other_values, me_ref)
+    held = (sent, left, plan, table, queries, keys, values, other_keys, other_values, me_ref)
     held = lax.optimization_barrier(held)
-    arrived, plan, table, queries, keys, values, other_keys, other_values, me_ref = held
+    arrived, left, plan, table, queries, keys, values, other_keys, other_values, me_ref = held
     arrived = arrived.reshape(CHIPS, SLOT_PIECES, PIECE, HEAD)
     pieces, *outgoing = forward(plan, me_ref, arrived)
     pieces = exchange(pieces)
@@ -619,7 +621,7 @@
         )
     out = out.reshape(BLOCK, HEADS * HEAD)
     return lax.cond(
-        plan[ROW_LEFT, 0] > 0,
+        left[0] > 0,
         lambda: full_attention(queries, keys, values, chosen_all, me),
         lambda: out,
     )

time: 328 us -> 323 us (0.985); the launches traced: 328 us -> 317 us
  waiting for transfers between devices: 11.6 us -> 7.91 us
    ppermute x13, waiting for transfers between devices: 3.75 us -> 0.03 us  [body(): lax.ppermute(outgoing[kind], 'ctx', shift_pairs(SHIFTS[kind]))]
    ppermute x13, starting transfers between devices: 26.4 us -> 22.7 us  [body(): lax.ppermute(outgoing[kind], 'ctx', shift_pairs(SHIFTS[kind]))]
  transfers between devices with their start and end apart: 17 -> 17, of which waited for: 2 -> 1; matrix products, arithmetic and copies ran while one was open for 1% -> 0% of each run, Pallas kernels for 9% -> 12%
where the time goes in v3:
time: 323 us; the launch traced here: 317 us
  blocking collectives  204 us (63%)
  Pallas kernels  58.3 us (18%)
  starting transfers between devices  41.8 us (13%)
  waiting for transfers between devices  7.91 us (2%)
  local copies, waits for them, and re-layouts  3.96 us (1%)
    all_to_all x1, blocking collectives, exchange(): lax.all_to_all(array, 'ctx', 0, 0, axis_index_groups=LANES, tiled=True)  204 us
    pallas_call x4, Pallas kernels, attend(): pl.pallas_call(lambda *refs: attend_kernel(wave, kinds, *refs), in_specs=...  37.7 us
    ppermute x13, starting transfers between devices, body(): lax.ppermute(outgoing[kind], 'ctx', shift_pairs(SHIFTS[kind]))  22.7 us
    pallas_call x1, Pallas kernels, pack(): pl.pallas_call(pack_kernel, in_specs=[VMEM, SMEM, ANY, ANY, ANY, ANY], ou...  13.3 us
    all_to_all x1, starting transfers between devices, body(): chosen_all = lax.all_to_all(spread, 'ctx', 0, 0, tiled=True)  10.6 us
    all_to_all x1, waiting for transfers between devices, body(): chosen_all = lax.all_to_all(spread, 'ctx', 0, 0, tiled=True)  7.87 us
    all_to_all x1, starting transfers between devices, exchange(): lax.all_to_all(array, 'ctx', 0, 0, axis_index_groups=LANES, tiled=True)  7.77 us
    pallas_call x1, Pallas kernels, forward(): pl.pallas_call(forward_kernel, in_specs=[SMEM, SMEM, ANY], out_specs=[ANY...  7.22 us
  transfers between devices with their start and end apart: 17, of which 1 were waited for; matrix products, arithmetic and copies ran while one was open for 0% of the time, Pallas kernels for 12%

profile of v3, /device:TPU:7, one launch (start us, length us, event | category | flops | bytes accessed | tf_op | source)
XLA Modules:
  0.0 317.3 jit_solution(611636346722521258)
XLA Ops:
  0.0 0.7 collective-permute-start
  0.7 0.0 collective-permute-start.1
  0.7 0.8 copy.30
  1.4 0.1 broadcast_in_dim.55
  1.5 0.7 broadcast_in_dim.56
  2.2 10.6 %all-to-all-start.2 = ((s32[128,1,48]{2,1,0:T(1,128)}), s32[128,1,48]{2,1,0:T(1,128)S(1)}, u32[]{:S(2)}, u32[]{:S(2)}) async-start(s32[128,1,48]{2,1,0:T(1,128)} %broadcast_in_dim.56), calls=%async_computation.2 | async-start | bytes 131072 | tf_op jit(solution)/shard_map/all_to_all | solution.py:594
  12.8 7.9 %all-to-all-done.2 = s32[128,1,48]{2,1,0:T(1,128)S(1)} async-done(((s32[128,1,48]{2,1,0:T(1,128)}), s32[128,1,48]{2,1,0:T(1,128)S(1)}, u32[]{:S(2)}, u32[]{:S(2)}) %all-to-all-start.2) | async-done | bytes 24608 | tf_op jit(solution)/shard_map/all_to_all | solution.py:594
  20.7 0.1 copy.31
  20.8 0.0 collective-permute-done
  20.8 0.0 copy-start.3
  20.8 0.0 collective-permute-done.1
  20.8 1.3 copy-done.3
  22.1 13.3 %pack.1 = (s32[248,128]{1,0:T(8,128)}, bf16[32,2,69,16,128]{4,3,2,1,0:T(8,128)(2,1)}, s32[148]{0:T(256)}, s32[1]{0:T(128)}) custom-call(s32[48,128]{1,0:T(8,128)S(1)} %bitcast.100, s32[1]{0:T(128)} %bitcast.13.me_ref, bf16[32,16,2048]{2,1,0:T(8,128)(2,1)} %bitcast.73, bf16[32,16,2048]{2,1,0:T(8,128)(2,1)} %bitcast.78, bf16[32,16,2048]{2,1,0:T(8,128)(2,1)} %bitcast.83, ...), custom_call_target="tpu_custom_call" | custom-call | tf_op jit(solution)/shard_map/pack/pallas_call | solution.py:295
  35.4 204.4 %all_to_all.28 = bf16[64,1104,128]{2,1,0:T(8,128)(2,1)} all-to-all(bf16[64,1104,128]{2,1,0:T(8,128)(2,1)} %bitcast.93), channel_id=1, replica_groups={{0,32,64,96,8,40,72,104,16,48,80,112,24,56,88,120,2,34,66,98,10,42,74,1..., dimensions={0} | all-to-all | bytes 36175872 | tf_op jit(solution)/shard_map/all_to_all | solution.py:558
  239.9 0.0 copy-start.1
  239.9 7.2 %forward.1 = (bf16[64,5,16,128]{3,2,1,0:T(8,128)(2,1)}, bf16[6,64,16,128]{3,2,1,0:T(8,128)(2,1)}, bf16[1,64,16,128]{3,2,1,0:T(8,128)(2,1)}, bf16[1,64,16,128]{3,...) custom-call(s32[248,128]{1,0:T(8,128)} %get-tuple-element.192.plan, ...), custom_call_target="tpu_custom_call" | custom-call | tf_op jit(solution)/shard_map/forward/pallas_call | solution.py:372
  247.1 2.9 collective-permute-start.2
  250.0 0.6 collective-permute-start.3
  250.6 0.9 collective-permute-start.4
  251.5 4.5 %collective-permute-start.5 = (bf16[1,64,16,128]{3,2,1,0:T(8,128)(2,1)}, bf16[1,64,16,128]{3,2,1,0:T(8,128)(2,1)}, u32[]{:S(2)}, u32[]{:S(2)}) collective-permute-start(bf16[1,64,16,128]{3,2,1,0:T(8,128)(2,1)} %get-tuple-element.197), channel_id=1, source_target_pairs={{8,0},{9,1},{10,2},{11,3},{12,4},{13,5},{14,6},{15,7},{16,8},{17,9... | collective-permute-start | bytes 786440 | tf_op jit(solution)/shard_map/ppermute | solution.py:609
  256.0 0.0 collective-permute-start.6
  256.0 7.8 %all-to-all-start.4 = ((bf16[64,5,16,128]{3,2,1,0:T(8,128)(2,1)}), bf16[64,5,16,128]{3,2,1,0:T(8,128)(2,1)S(1)}, u32[]{:S(2)}, u32[]{:S(2)}) async-start(bf16[64,5,16,128]{3,2,1,0:T(8,128)(2,1)} %get-tuple-element.207), calls=%async_computation.4 | async-start | bytes 2621440 | tf_op jit(solution)/shard_map/all_to_all | solution.py:558
  263.8 0.0 copy-done.1
  263.8 16.9 %attend.4.refs_12_ = bf16[32,16,2048]{2,1,0:T(8,128)(2,1)} custom-call(s32[148]{0:T(256)} %get-tuple-element.185.refs_0_, bf16[32,16,2048]{2,1,0:T(8,128)(2,1)} %bitcast.88, bf16[32,16,2048]{2,1,0:T(8,128)(2,1)S(1)} %bitcast.74, bf16[32,16,2048]{2,1,0:T(8,128)(2,1)} %bitcast.79, bf16[32,16,2048]{2,1,0:T(8,128)(2,1)} %bitcast.84, ...), custom_call_target="tpu_custom_call" | custom-call | flops 19327352832 | bytes 3145728 | tf_op jit(solution)/shard_map/attend/pallas_call | solution.py:531
  281.3 0.0 collective-permute-done.3.refs_8_
  281.3 1.1 collective-permute-start.10
  282.4 0.0 collective-permute-done.4.refs_9_
  282.4 4.5 %collective-permute-start.7 = (bf16[1,64,16,128]{3,2,1,0:T(8,128)(2,1)}, bf16[1,64,16,128]{3,2,1,0:T(8,128)(2,1)S(1)}, u32[]{:S(2)}, u32[]{:S(2)}) collective-permute-start(bf16[1,64,16,128]{3,2,1,0:T(8,128)(2,1)} %get-tuple-element.199), channel_id=1, source_target_pairs={{2,0},{3,1},{4,2},{5,3},{6,4},{7,5},{0,6},{1,7},{10,8},{11,9},{12,... | collective-permute-start | bytes 786440 | tf_op jit(solution)/shard_map/ppermute | solution.py:609
  286.9 0.0 collective-permute-done.5.refs_10_
  286.9 0.0 collective-permute-start.8
  286.9 0.0 collective-permute-done.6.refs_11_
  286.9 1.7 collective-permute-start.9
  288.5 0.0 collective-permute-done.2.refs_7_
  288.5 0.7 collective-permute-start.11
  289.3 10.1 %attend.5.refs_16_ = bf16[32,16,2048]{2,1,0:T(8,128)(2,1)} custom-call(s32[148]{0:T(256)} %get-tuple-element.185.refs_0_, bf16[32,16,2048]{2,1,0:T(8,128)(2,1)} %bitcast.89, bf16[32,16,2048]{2,1,0:T(8,128)(2,1)S(1)} %bitcast.75, bf16[32,16,2048]{2,1,0:T(8,128)(2,1)} %bitcast.80, bf16[32,16,2048]{2,1,0:T(8,128)(2,1)} %bitcast.85, ...), custom_call_target="tpu_custom_call", output_to_operand_aliasing={{}: (12, {})} | custom-call | flops 8589934592 | bytes 3145728 | tf_op jit(solution)/shard_map/attend/pallas_call | solution.py:531
  299.3 0.0 collective-permute-done.10.refs_15_
  299.4 0.0 copy-start.5
  299.4 4.1 %collective-permute-start.12 = (bf16[1,64,16,128]{3,2,1,0:T(8,128)(2,1)}, bf16[1,64,16,128]{3,2,1,0:T(8,128)(2,1)}, u32[]{:S(2)}, u32[]{:S(2)}) collective-permute-start(bf16[1,64,16,128]{3,2,1,0:T(8,128)(2,1)} %get-tuple-element.204), channel_id=1, source_target_pairs={{25,0},{24,1},{27,2},{26,3},{29,4},{28,5},{31,6},{30,7},{1,8},{0,9... | collective-permute-start | bytes 786440 | tf_op jit(solution)/shard_map/ppermute | solution.py:609
  303.5 0.0 collective-permute-done.7.refs_12_
  303.5 0.0 copy-start.6
  303.5 0.9 collective-permute-start.13
  304.4 0.0 collective-permute-done.8.refs_13_
  304.5 0.8 collective-permute-start.14
  305.3 0.0 collective-permute-done.9.refs_14_
  305.3 0.0 copy-done.5
  305.3 0.0 copy-done.6
  305.3 9.9 %attend.6.refs_21_ = bf16[32,16,2048]{2,1,0:T(8,128)(2,1)} custom-call(s32[148]{0:T(256)} %get-tuple-element.185.refs_0_, bf16[32,16,2048]{2,1,0:T(8,128)(2,1)} %bitcast.90, bf16[32,16,2048]{2,1,0:T(8,128)(2,1)S(1)} %bitcast.76, bf16[32,16,2048]{2,1,0:T(8,128)(2,1)} %bitcast.81, bf16[32,16,2048]{2,1,0:T(8,128)(2,1)} %bitcast.86, ...), custom_call_target="tpu_custom_call", output_to_operand_aliasing={{}: (16, {})} | custom-call | flops 4294967296 | bytes 3145728 | tf_op jit(solution)/shard_map/attend/pallas_call | solution.py:531
  315.2 0.0 collective-permute-done.11.refs_16_
  315.2 0.0 collective-permute-done.12.refs_17_
  315.2 0.0 collective-permute-done.13.refs_18_
  315.2 0.0 collective-permute-done.14.refs_19_
  315.2 0.0 all-to-all-done.4
  315.2 0.0 copy-start.4
  315.2 1.1 copy-done.4
  316.3 0.9 attend.7
  (1 shorter events, 0.0 us)
Async XLA Ops:
  0.0 20.8 %collective-permute-start = (bf16[512,2048]{1,0:T(8,128)(2,1)}, bf16[512,2048]{1,0:T(8,128)(2,1)S(1)}, u32[]{:S(2)}, u32[]{:S(2)}) collective-permute-start(bf16[512,2048]{1,0:T(8,128)(2,1)} %param.11), channel_id=1, source_target_pairs={{0,1},{1,0},{2,3},{3,2},{4,5},{5,4},{6,7},{7,6},{8,9},{9,8},{10,11... | collective-permute-start | bytes 6291464 | tf_op jit(solution)/shard_map/ppermute | solution.py:591
  0.7 20.1 %collective-permute-start.1 = (bf16[512,2048]{1,0:T(8,128)(2,1)}, bf16[512,2048]{1,0:T(8,128)(2,1)}, u32[]{:S(2)}, u32[]{:S(2)}) collective-permute-start(bf16[512,2048]{1,0:T(8,128)(2,1)} %param.12), channel_id=1, source_target_pairs={{0,1},{1,0},{2,3},{3,2},{4,5},{5,4},{6,7},{7,6},{8,9},{9,8},{10,11... | collective-permute-start | bytes 6291464 | tf_op jit(solution)/shard_map/ppermute | solution.py:592
  2.2 18.5 %all-to-all-start.2 = ((s32[128,1,48]{2,1,0:T(1,128)}), s32[128,1,48]{2,1,0:T(1,128)S(1)}, u32[]{:S(2)}, u32[]{:S(2)}) async-start(s32[128,1,48]{2,1,0:T(1,128)} %broadcast_in_dim.56), calls=%async_computation.2 | async-start | bytes 131072 | tf_op jit(solution)/shard_map/all_to_all | solution.py:594
  20.8 1.3 copy-start.3
  239.9 23.9 %copy-start.1 = (bf16[512,2048]{1,0:T(8,128)(2,1)S(1)}, bf16[512,2048]{1,0:T(8,128)(2,1)}, u32[]{:S(2)}) copy-start(bf16[512,2048]{1,0:T(8,128)(2,1)} %param.11) | copy-start | bytes 6291460
  247.1 41.4 %collective-permute-start.2 = (bf16[6,64,16,128]{3,2,1,0:T(8,128)(2,1)}, bf16[6,64,16,128]{3,2,1,0:T(8,128)(2,1)}, u32[]{:S(2)}, u32[]{:S(2)}) collective-permute-start(bf16[6,64,16,128]{3,2,1,0:T(8,128)(2,1)} %get-tuple-element.194), channel_id=1, source_target_pairs={{1,0},{0,1},{3,2},{2,3},{5,4},{4,5},{7,6},{6,7},{9,8},{8,9},{11,10... | collective-permute-start | bytes 4718600 | tf_op jit(solution)/shard_map/ppermute | solution.py:609
  250.0 31.3 %collective-permute-start.3 = (bf16[1,64,16,128]{3,2,1,0:T(8,128)(2,1)}, bf16[1,64,16,128]{3,2,1,0:T(8,128)(2,1)}, u32[]{:S(2)}, u32[]{:S(2)}) collective-permute-start(bf16[1,64,16,128]{3,2,1,0:T(8,128)(2,1)} %get-tuple-element.195), channel_id=1, source_target_pairs={{32,0},{33,1},{34,2},{35,3},{36,4},{37,5},{38,6},{39,7},{40,8},{41... | collective-permute-start | bytes 786440 | tf_op jit(solution)/shard_map/ppermute | solution.py:609
  250.6 31.8 %collective-permute-start.4 = (bf16[1,64,16,128]{3,2,1,0:T(8,128)(2,1)}, bf16[1,64,16,128]{3,2,1,0:T(8,128)(2,1)}, u32[]{:S(2)}, u32[]{:S(2)}) collective-permute-start(bf16[1,64,16,128]{3,2,1,0:T(8,128)(2,1)} %get-tuple-element.196), channel_id=1, source_target_pairs={{96,0},{97,1},{98,2},{99,3},{100,4},{101,5},{102,6},{103,7},{104,8... | collective-permute-start | bytes 786440 | tf_op jit(solution)/shard_map/ppermute | solution.py:609
  251.5 35.4 %collective-permute-start.5 = (bf16[1,64,16,128]{3,2,1,0:T(8,128)(2,1)}, bf16[1,64,16,128]{3,2,1,0:T(8,128)(2,1)}, u32[]{:S(2)}, u32[]{:S(2)}) collective-permute-start(bf16[1,64,16,128]{3,2,1,0:T(8,128)(2,1)} %get-tuple-element.197), channel_id=1, source_target_pairs={{8,0},{9,1},{10,2},{11,3},{12,4},{13,5},{14,6},{15,7},{16,8},{17,9... | collective-permute-start | bytes 786440 | tf_op jit(solution)/shard_map/ppermute | solution.py:609
  256.0 30.9 %collective-permute-start.6 = (bf16[1,64,16,128]{3,2,1,0:T(8,128)(2,1)}, bf16[1,64,16,128]{3,2,1,0:T(8,128)(2,1)}, u32[]{:S(2)}, u32[]{:S(2)}) collective-permute-start(bf16[1,64,16,128]{3,2,1,0:T(8,128)(2,1)} %get-tuple-element.198), channel_id=1, source_target_pairs={{24,0},{25,1},{26,2},{27,3},{28,4},{29,5},{30,6},{31,7},{0,8},{1,9... | collective-permute-start | bytes 786440 | tf_op jit(solution)/shard_map/ppermute | solution.py:609
  256.0 59.2 %all-to-all-start.4 = ((bf16[64,5,16,128]{3,2,1,0:T(8,128)(2,1)}), bf16[64,5,16,128]{3,2,1,0:T(8,128)(2,1)S(1)}, u32[]{:S(2)}, u32[]{:S(2)}) async-start(bf16[64,5,16,128]{3,2,1,0:T(8,128)(2,1)} %get-tuple-element.207), calls=%async_computation.4 | async-start | bytes 2621440 | tf_op jit(solution)/shard_map/all_to_all | solution.py:558
  281.3 18.1 %collective-permute-start.10 = (bf16[1,64,16,128]{3,2,1,0:T(8,128)(2,1)}, bf16[1,64,16,128]{3,2,1,0:T(8,128)(2,1)S(1)}, u32[]{:S(2)}, u32[]{:S(2)}) collective-permute-start(bf16[1,64,16,128]{3,2,1,0:T(8,128)(2,1)} %get-tuple-element.202), channel_id=1, source_target_pairs={{97,0},{96,1},{99,2},{98,3},{101,4},{100,5},{103,6},{102,7},{105,8... | collective-permute-start | bytes 786440 | tf_op jit(solution)/shard_map/ppermute | solution.py:609
  282.4 21.1 %collective-permute-start.7 = (bf16[1,64,16,128]{3,2,1,0:T(8,128)(2,1)}, bf16[1,64,16,128]{3,2,1,0:T(8,128)(2,1)S(1)}, u32[]{:S(2)}, u32[]{:S(2)}) collective-permute-start(bf16[1,64,16,128]{3,2,1,0:T(8,128)(2,1)} %get-tuple-element.199), channel_id=1, source_target_pairs={{2,0},{3,1},{4,2},{5,3},{6,4},{7,5},{0,6},{1,7},{10,8},{11,9},{12,... | collective-permute-start | bytes 786440 | tf_op jit(solution)/shard_map/ppermute | solution.py:609
  286.9 17.6 %collective-permute-start.8 = (bf16[1,64,16,128]{3,2,1,0:T(8,128)(2,1)}, bf16[1,64,16,128]{3,2,1,0:T(8,128)(2,1)}, u32[]{:S(2)}, u32[]{:S(2)}) collective-permute-start(bf16[1,64,16,128]{3,2,1,0:T(8,128)(2,1)} %get-tuple-element.200), channel_id=1, source_target_pairs={{6,0},{7,1},{0,2},{1,3},{2,4},{3,5},{4,6},{5,7},{14,8},{15,9},{8,1... | collective-permute-start | bytes 786440 | tf_op jit(solution)/shard_map/ppermute | solution.py:609
  286.9 18.4 %collective-permute-start.9 = (bf16[1,64,16,128]{3,2,1,0:T(8,128)(2,1)}, bf16[1,64,16,128]{3,2,1,0:T(8,128)(2,1)}, u32[]{:S(2)}, u32[]{:S(2)}) collective-permute-start(bf16[1,64,16,128]{3,2,1,0:T(8,128)(2,1)} %get-tuple-element.201), channel_id=1, source_target_pairs={{33,0},{32,1},{35,2},{34,3},{37,4},{36,5},{39,6},{38,7},{41,8},{40... | collective-permute-start | bytes 786440 | tf_op jit(solution)/shard_map/ppermute | solution.py:609
  288.5 26.6 %collective-permute-start.11 = (bf16[1,64,16,128]{3,2,1,0:T(8,128)(2,1)}, bf16[1,64,16,128]{3,2,1,0:T(8,128)(2,1)}, u32[]{:S(2)}, u32[]{:S(2)}) collective-permute-start(bf16[1,64,16,128]{3,2,1,0:T(8,128)(2,1)} %get-tuple-element.203), channel_id=1, source_target_pairs={{9,0},{8,1},{11,2},{10,3},{13,4},{12,5},{15,6},{14,7},{17,8},{16,9... | collective-permute-start | bytes 786440 | tf_op jit(solution)/shard_map/ppermute | solution.py:609
  299.4 5.9 %copy-start.5 = (bf16[1,64,16,128]{3,2,1,0:T(8,128)(2,1)}, bf16[1,64,16,128]{3,2,1,0:T(8,128)(2,1)S(1)}, u32[]{:S(2)}) copy-start(bf16[1,64,16,128]{3,2,1,0:T(8,128)(2,1)S(1)} %collective-permute-done.10.refs_15_) | copy-start | bytes 786436
  299.4 15.8 %collective-permute-start.12 = (bf16[1,64,16,128]{3,2,1,0:T(8,128)(2,1)}, bf16[1,64,16,128]{3,2,1,0:T(8,128)(2,1)}, u32[]{:S(2)}, u32[]{:S(2)}) collective-permute-start(bf16[1,64,16,128]{3,2,1,0:T(8,128)(2,1)} %get-tuple-element.204), channel_id=1, source_target_pairs={{25,0},{24,1},{27,2},{26,3},{29,4},{28,5},{31,6},{30,7},{1,8},{0,9... | collective-permute-start | bytes 786440 | tf_op jit(solution)/shard_map/ppermute | solution.py:609
  303.5 1.8 copy-start.6
  303.5 11.7 %collective-permute-start.13 = (bf16[1,64,16,128]{3,2,1,0:T(8,128)(2,1)}, bf16[1,64,16,128]{3,2,1,0:T(8,128)(2,1)}, u32[]{:S(2)}, u32[]{:S(2)}) collective-permute-start(bf16[1,64,16,128]{3,2,1,0:T(8,128)(2,1)} %get-tuple-element.205), channel_id=1, source_target_pairs={{3,0},{2,1},{5,2},{4,3},{7,4},{6,5},{1,6},{0,7},{11,8},{10,9},{13,... | collective-permute-start | bytes 786440 | tf_op jit(solution)/shard_map/ppermute | solution.py:609
  304.5 10.7 %collective-permute-start.14 = (bf16[1,64,16,128]{3,2,1,0:T(8,128)(2,1)}, bf16[1,64,16,128]{3,2,1,0:T(8,128)(2,1)}, u32[]{:S(2)}, u32[]{:S(2)}) collective-permute-start(bf16[1,64,16,128]{3,2,1,0:T(8,128)(2,1)} %get-tuple-element.206), channel_id=1, source_target_pairs={{7,0},{6,1},{1,2},{0,3},{3,4},{2,5},{5,6},{4,7},{15,8},{14,9},{9,1... | collective-permute-start | bytes 786440 | tf_op jit(solution)/shard_map/ppermute | solution.py:609
  315.2 1.1 copy-start.4
